TPU v7x, 256 devices: a whole 4x4x8 slice. The times are simulated.
256 devices in a mesh: seq: 64 (over x, y_lo, z), outer: 4 (over y_hi, core).
Axes of the slice: x: 4, y: 4 (y_hi: 2, y_lo: 2; y = y_hi * 2 + y_lo), z: 8, core: 2. Of those that a mesh axis runs over, the one named last changes fastest.
Arguments:
- queries: bfloat16 [65536, 1024], P(('seq', 'outer')), may hold values from -120 to 120
- keys: bfloat16 [65536, 1024], P(('seq', 'outer')), may hold values from -10 to 10
- values: bfloat16 [65536, 1024], P(('seq', 'outer')), may hold values from -10 to 10
- cotangent: bfloat16 [65536, 1024], P(('seq', 'outer')), may hold values from -6 to 6
Outputs:
- attended: bfloat16 [65536, 1024], P(('seq', 'outer'))
- grad_queries: float32 [65536, 1024], P(('seq', 'outer'))
- grad_keys: float32 [65536, 1024], P(('seq', 'outer'))
- grad_values: float32 [65536, 1024], P(('seq', 'outer'))
- summary_grad: float32 [256, 2048], P(('seq', 'outer'))
All inputs are finite; a program needn't handle non-finite values.
Results may differ from a plain program's by a relative error of at most 0.01.
Values may be sent and summed in bfloat16 or wider, within the bound.
A program may use at most 128 MiB of HBM per device.

v0:
```python
import jax
import jax.numpy as jnp
from jax import lax
from jax.sharding import PartitionSpec as P

HEADS = 8


def with_halo(cells, sides, width):
    for axis, dim in sides:
        count = lax.axis_size(axis)
        ends = count - 1
        head = lax.slice_in_dim(cells, 0, width, axis=dim)
        tail = lax.slice_in_dim(cells, cells.shape[dim] - width, cells.shape[dim], axis=dim)
        cells = jnp.concatenate(
            [
                lax.ppermute(tail, axis, [(i, (i + 1) % count) for i in range(ends)]),
                cells,
                lax.ppermute(head, axis, [((i + 1) % count, i) for i in range(ends)]),
            ],
            axis=dim,
        )
    return cells


def swapped(value, axis, stride):
    mask = 2**stride
    pairs = [(source, source ^ mask) for source in range(lax.axis_size(axis))]
    return lax.ppermute(value, axis, pairs)


def halved(matrix):
    return (
        jnp.sum(matrix.reshape(matrix.shape[0] // 2, 2, matrix.shape[1]), axis=1, dtype=jnp.float32)
        * 0.5
    ).astype(jnp.bfloat16)


def doubled(matrix):
    return jnp.broadcast_to(matrix[:, None, :], (matrix.shape[0], 2, matrix.shape[1])).reshape(
        2 * matrix.shape[0], matrix.shape[1]
    )


def attend(query_rows, key_sets, usable, cotangent):
    leaf_count, set_size, double_width = key_sets.shape
    feat_width = double_width // 2
    head_size = feat_width // HEADS
    leaf_rows = query_rows.shape[0] // leaf_count
    queries_h = query_rows.reshape(leaf_count, leaf_rows, HEADS, head_size)
    keys_h = key_sets[:, :, :feat_width].reshape(leaf_count, set_size, HEADS, head_size)
    values_h = key_sets[:, :, feat_width:].reshape(leaf_count, set_size, HEADS, head_size)
    cot_h = cotangent.reshape(leaf_count, leaf_rows, HEADS, head_size)
    score_scale = head_size ** (-0.5)
    scores = (
        jnp.einsum("bqhe,bkhe->bhqk", queries_h, keys_h, preferred_element_type=jnp.float32)
        * score_scale
    )
    scores = jnp.where(usable[:, None, None, :], scores, -jnp.inf)
    highest = jnp.max(scores, axis=-1, keepdims=True)
    weights = jnp.exp(scores - highest)
    probs = weights / jnp.sum(weights, axis=-1, keepdims=True)
    probs_low = probs.astype(jnp.bfloat16)
    attended = jnp.einsum(
        "bhqk,bkhe->bqhe", probs_low, values_h, preferred_element_type=jnp.float32
    )
    dprobs = jnp.einsum("bqhe,bkhe->bhqk", cot_h, values_h, preferred_element_type=jnp.float32)
    centre = jnp.sum(probs * dprobs, axis=-1, keepdims=True)
    dscores = (probs * (dprobs - centre)).astype(jnp.bfloat16)
    grad_q = (
        jnp.einsum("bhqk,bkhe->bqhe", dscores, keys_h, preferred_element_type=jnp.float32)
        * score_scale
    )
    grad_k = (
        jnp.einsum("bhqk,bqhe->bkhe", dscores, queries_h, preferred_element_type=jnp.float32)
        * score_scale
    )
    grad_v = jnp.einsum("bhqk,bqhe->bkhe", probs_low, cot_h, preferred_element_type=jnp.float32)
    total_rows = leaf_count * leaf_rows
    set_grad = jnp.concatenate(
        [
            grad_k.reshape(leaf_count, set_size, feat_width),
            grad_v.reshape(leaf_count, set_size, feat_width),
        ],
        axis=-1,
    )
    return (
        attended.reshape(total_rows, feat_width).astype(jnp.bfloat16),
        grad_q.reshape(total_rows, feat_width),
        set_grad,
    )


def on_device(queries, keys, values, cotangent):
    dev_rows = queries.shape[0]
    leaf_rows = dev_rows // 2
    half_rows = leaf_rows // 2
    span_count = lax.axis_size(("seq", "outer"))
    position = lax.axis_index(("seq", "outer"))
    is_odd = position % 2 == 1
    keyvals = jnp.concatenate([keys, values], axis=1)
    pairs = halved(keyvals)
    own_quads = halved(pairs)
    summary = (jnp.sum(keyvals, axis=0, keepdims=True, dtype=jnp.float32) / dev_rows).astype(
        jnp.bfloat16
    )
    extended_kv = with_halo(keyvals, ((("seq", "outer"), 0),), leaf_rows)
    left_rim = extended_kv[:leaf_rows]
    right_rim = extended_kv[dev_rows + leaf_rows :]
    partner_pairs = swapped(pairs, ("seq", "outer"), 0)
    partner_quads = halved(partner_pairs)
    pair_quads = jnp.where(
        is_odd,
        jnp.concatenate([partner_quads, own_quads], axis=0),
        jnp.concatenate([own_quads, partner_quads], axis=0),
    )
    sibling_quads = swapped(pair_quads, ("seq", "outer"), 1)
    all_summaries = lax.all_gather(summary, ("seq", "outer"), axis=0, tiled=True)
    far_keys = jnp.concatenate([partner_pairs, sibling_quads, all_summaries], axis=0)
    local_ext = jnp.concatenate([left_rim, keyvals, right_rim], axis=0)
    near_keys = jnp.stack([local_ext[: 3 * leaf_rows], local_ext[leaf_rows:]])
    key_sets = jnp.concatenate(
        [near_keys, jnp.broadcast_to(far_keys[None], (2,) + far_keys.shape)], axis=1
    )
    slots = jnp.arange(key_sets.shape[1], dtype=jnp.int32)
    covered = (slots >= 5 * leaf_rows) & ((slots - 5 * leaf_rows) // 4 == position // 4)
    usable = jnp.stack(
        [
            ((slots >= leaf_rows) | (position > 0)) & ~covered,
            ((slots < 2 * leaf_rows) | (slots >= 3 * leaf_rows) | (position < span_count - 1))
            & ~covered,
        ]
    )
    attended, grad_q, set_grad = attend(queries, key_sets, usable, cotangent)
    ext_grad = jnp.pad(set_grad[0, : 3 * leaf_rows], ((0, leaf_rows), (0, 0))) + jnp.pad(
        set_grad[1, : 3 * leaf_rows], ((leaf_rows, 0), (0, 0))
    )
    far_grad = set_grad[0, 3 * leaf_rows :] + set_grad[1, 3 * leaf_rows :]
    partner_grad = far_grad[:leaf_rows]
    sibling_grad = far_grad[leaf_rows : 2 * leaf_rows]
    summary_terms = far_grad[2 * leaf_rows :]
    pair_grad = swapped(sibling_grad.astype(jnp.bfloat16), ("seq", "outer"), 1).astype(
        sibling_grad.dtype
    )
    own_half = jnp.where(is_odd, pair_grad[half_rows:], pair_grad[:half_rows])
    other_half = jnp.where(is_odd, pair_grad[:half_rows], pair_grad[half_rows:])
    outgoing = partner_grad + 0.5 * doubled(other_half)
    left_grad = ext_grad[:leaf_rows]
    own_grad = ext_grad[leaf_rows : 3 * leaf_rows]
    right_grad = ext_grad[3 * leaf_rows :]
    returned = with_halo(
        jnp.concatenate([left_grad, right_grad], axis=0).astype(jnp.bfloat16),
        ((("seq", "outer"), 0),),
        leaf_rows,
    ).astype(jnp.float32)
    from_prev = returned[:leaf_rows]
    from_next = returned[3 * leaf_rows :]
    incoming = swapped(outgoing.astype(jnp.bfloat16), ("seq", "outer"), 0).astype(outgoing.dtype)
    pairs_total = incoming + 0.5 * doubled(own_half)
    summary_grad = lax.psum_scatter(
        summary_terms, ("seq", "outer"), scatter_dimension=0, tiled=True
    )
    zero_block = jnp.zeros_like(from_prev)
    token_grad = (
        own_grad
        + jnp.concatenate([from_prev, zero_block], axis=0)
        + jnp.concatenate([zero_block, from_next], axis=0)
    )
    token_grad = token_grad + 0.5 * doubled(pairs_total) + summary_grad / dev_rows
    feat_width = queries.shape[1]
    return (attended, grad_q, token_grad[:, :feat_width], token_grad[:, feat_width:], summary_grad)


def solution(mesh):
    in_specs = (
        P(("seq", "outer"), None),
        P(("seq", "outer"), None),
        P(("seq", "outer"), None),
        P(("seq", "outer"), None),
    )
    out_specs = (
        P(("seq", "outer"), None),
        P(("seq", "outer"), None),
        P(("seq", "outer"), None),
        P(("seq", "outer"), None),
        P(("seq", "outer"), None),
    )
    return jax.shard_map(
        on_device, mesh=mesh, in_specs=in_specs, out_specs=out_specs, check_vma=False
    )
```

profile of v0, /device:TPU:1, one launch (start us, length us, event | category | flops | bytes accessed | tf_op | source)
XLA Modules:
  0.0 783.8 jit_solution(3173445426228822557)
XLA Ops:
  16.4 4.2 reduce_sum.54
  20.7 3.3 collective-permute-start.2
  25.1 3.0 collective-permute-start
  44.9 3.2 maximum_bitcast_fusion.2
  48.2 354.6 %all-gather.3.cloned.1.call-done = bf16[524288]{0:T(1024)(128)(2,1)} async-done(((bf16[2048]{0:T(1024)(128)(2,1)}), bf16[524288]{0:T(1024)(128)(2,1)}) %all-gather.3.cloned.1.call-update) | async-done | bytes 1048592 | tf_op jit(solution)/shard_map/all_gather | solution.py:118
  404.3 2.5 pad_maximum_fusion.2
  406.8 2.9 copy.66
  412.5 3.5 fusion.40
  416.0 8.1 %fusion.43 = (f32[2,8,128]{2,1,0:T(8,128)S(1)}, f32[2,8,128,896]{2,3,1,0:T(8,128)}) fusion(pred[2,896]{1,0:T(4,128)(4,1)S(1)} %pad_add_fusion.1, bf16[2,896,8,128]{1,3,2,0:T(8,128)(2,1)} %bitcast.82, bf16[2,128,8,128]{1,3,2,0:T(8,128)(2,1)S(1)} %copy.76), kind=kOutput, calls=%fused_computation.85 | convolution fusion | flops 477102976 | bytes 11544320 | tf_op jit(solution)/shard_map/sub | solution.py:61
  424.1 6.3 fusion.26
  431.6 4.5 fusion.1
  436.1 4.3 fusion.18
  440.4 6.6 fusion.3
  449.1 4.0 multiply_bitcast_fusion
  453.2 8.1 %copy.82 = f32[2,896,1024]{2,1,0:T(8,128)} copy(f32[2,896,1024]{1,2,0:T(8,128)} %bitcast.84) | data formatting | bytes 14680064 | tf_op jit(solution)/shard_map/reshape | solution.py:83
  461.2 8.1 %copy.78 = f32[2,896,8,128]{1,3,2,0:T(8,128)} copy(f32[2,896,8,128]{3,1,2,0:T(8,128)} %multiply_bitcast_fusion) | data formatting | bytes 14680064 | tf_op jit(solution)/shard_map/mul | solution.py:75
  469.3 8.3 %copy.81 = f32[2,896,1024]{2,1,0:T(8,128)} copy(f32[2,896,1024]{1,2,0:T(8,128)} %bitcast.81) | data formatting | bytes 14680064 | tf_op jit(solution)/shard_map/reshape | solution.py:82
  477.6 4.4 fusion.9
  484.4 3.4 maximum_bitcast_fusion
  493.3 2.5 copy.74
  495.8 2.4 copy.96
  503.5 3.4 collective-permute-start.4
  508.9 4.7 collective-permute-done.6
  517.2 2.9 mul.79
  520.1 2.5 fusion.31
  523.8 2.6 broadcast_in_dim.24
  526.4 2.9 mul.81
  531.4 4.0 maximum_convert_fusion
  535.5 226.7 %all-reduce.6.cloned.1.call-done = f32[256,2048]{1,0:T(8,128)} async-done(((f32[256,2048]{1,0:T(8,128)}), f32[256,2048]{1,0:T(8,128)}) %all-reduce.6.cloned.1.call-update) | async-done | bytes 2097168
  765.1 2.5 broadcast_in_dim.25
  767.7 3.7 mul.83
  771.4 4.1 fusion.17
  (84 shorter events, 61.2 us)
Async XLA Ops:
  7.2 395.6 %all-gather.3.cloned.1.call-start = ((), (), s32[]{:S(2)}) async-start(), calls=%async_computation | async-start | bytes 1052672 | tf_op jit(solution)/shard_map/all_gather | solution.py:118
  10.7 751.5 %all-reduce.6.cloned.1.call-start = ((), (), s32[]{:S(2)}) async-start(), calls=%async_computation.1 | async-start | bytes 4194304
  16.4 14.4 %copy-start.8 = (bf16[256,1024]{1,0:T(8,128)(2,1)S(1)}, bf16[256,1024]{1,0:T(8,128)(2,1)}, u32[]{:S(2)}) copy-start(bf16[256,1024]{1,0:T(8,128)(2,1)} %param.4) | copy-start | bytes 1572868
  20.7 19.7 %collective-permute-start.2 = (bf16[128,2048]{1,0:T(8,128)(2,1)S(1)}, bf16[128,2048]{1,0:T(8,128)(2,1)}, u32[]{:S(2)}, u32[]{:S(2)}) collective-permute-start(bf16[128,2048]{1,0:T(8,128)(2,1)S(1)} %multiply_convert_fusion), channel_id=1, source_target_pairs={{0,1},{1,0},{2,3},{3,2},{4,5},{5,4},{6,7},{7,6},{8,9},{9,8},{10,11... | collective-permute-start | bytes 1572872 | tf_op jit(solution)/shard_map/ppermute | solution.py:29
  25.1 19.9 %collective-permute-start = (bf16[128,2048]{0,1:T(8,128)(2,1)}, bf16[128,2048]{0,1:T(8,128)(2,1)}, u32[]{:S(2)}, u32[]{:S(2)}) collective-permute-start(bf16[128,2048]{0,1:T(8,128)(2,1)} %get-tuple-element.19), channel_id=1, source_target_pairs={{0,1},{1,2},{2,3},{3,4},{4,5},{5,6},{6,7},{7,8},{8,9},{9,10},{10,1... | collective-permute-start | bytes 1572872 | tf_op jit(solution)/shard_map/ppermute | solution.py:17
  28.0 16.9 %collective-permute-start.1 = (bf16[128,2048]{0,1:T(8,128)(2,1)}, bf16[128,2048]{0,1:T(8,128)(2,1)}, u32[]{:S(2)}, u32[]{:S(2)}) collective-permute-start(bf16[128,2048]{0,1:T(8,128)(2,1)} %get-tuple-element.20), channel_id=1, source_target_pairs={{1,0},{2,1},{3,2},{4,3},{5,4},{6,5},{7,6},{8,7},{9,8},{10,9},{11,1... | collective-permute-start | bytes 1572872 | tf_op jit(solution)/shard_map/ppermute | solution.py:19
  43.6 360.7 %collective-permute-start.3 = (bf16[128,2048]{1,0:T(8,128)(2,1)S(1)}, bf16[128,2048]{1,0:T(8,128)(2,1)S(1)}, u32[]{:S(2)}, u32[]{:S(2)}) collective-permute-start(bf16[128,2048]{1,0:T(8,128)(2,1)S(1)} %maximum_select_fusion), channel_id=1, source_target_pairs={{0,2},{1,3},{2,0},{3,1},{4,6},{5,7},{6,4},{7,5},{8,10},{9,11},{10,... | collective-permute-start | bytes 1572872 | tf_op jit(solution)/shard_map/ppermute | solution.py:29
  409.7 1.4 copy-start.5
  409.7 1.9 copy-start.6
  424.1 6.3 copy-start.4
  424.1 7.5 copy-start.7
  424.1 7.5 copy-start.9
  440.4 6.6 copy-start.3
  469.3 12.7 %slice-start = ((s8[7340032]{0:T(1024)(128)(4,1)}), s8[3145728]{0:T(1024)(128)(4,1)S(1)}, s32[]{:S(2)}) async-start(s8[7340032]{0:T(1024)(128)(4,1)} %bitcast.79), calls=%async_computation.2 | async-start | bytes 6291456
  477.6 4.7 slice-start.1
  477.6 6.8 copy-start
  484.4 4.2 copy-start.2
  487.8 2.3 copy-start.10
  491.2 8.9 %copy-start.1 = (f32[384,2048]{1,0:T(8,128)S(1)}, f32[384,2048]{1,0:T(8,128)}, u32[]{:S(2)}) copy-start(f32[384,2048]{1,0:T(8,128)} %get-tuple-element.7) | copy-start | bytes 9437188
  498.2 15.4 %collective-permute-start.6 = (bf16[128,2048]{1,0:T(8,128)(2,1)}, bf16[128,2048]{1,0:T(8,128)(2,1)}, u32[]{:S(2)}, u32[]{:S(2)}) collective-permute-start(bf16[128,2048]{1,0:T(8,128)(2,1)} %fusion.32), channel_id=1, source_target_pairs={{0,2},{1,3},{2,0},{3,1},{4,6},{5,7},{6,4},{7,5},{8,10},{9,11},{10,... | collective-permute-start | bytes 1572872 | tf_op jit(solution)/shard_map/ppermute | solution.py:29
  503.5 25.8 %collective-permute-start.4 = (bf16[128,2048]{1,0:T(8,128)(2,1)}, bf16[128,2048]{1,0:T(8,128)(2,1)}, u32[]{:S(2)}, u32[]{:S(2)}) collective-permute-start(bf16[128,2048]{1,0:T(8,128)(2,1)} %get-tuple-element.13), channel_id=1, source_target_pairs={{0,1},{1,2},{2,3},{3,4},{4,5},{5,6},{6,7},{7,8},{8,9},{9,10},{10,1... | collective-permute-start | bytes 1572872 | tf_op jit(solution)/shard_map/ppermute | solution.py:17
  507.0 22.4 %collective-permute-start.5 = (bf16[128,2048]{1,0:T(8,128)(2,1)}, bf16[128,2048]{1,0:T(8,128)(2,1)}, u32[]{:S(2)}, u32[]{:S(2)}) collective-permute-start(bf16[128,2048]{1,0:T(8,128)(2,1)} %get-tuple-element.14), channel_id=1, source_target_pairs={{1,0},{2,1},{3,2},{4,3},{5,4},{6,5},{7,6},{8,7},{9,8},{10,9},{11,1... | collective-permute-start | bytes 1572872 | tf_op jit(solution)/shard_map/ppermute | solution.py:19
  522.6 241.1 %collective-permute-start.7 = (bf16[128,2048]{1,0:T(8,128)(2,1)}, bf16[128,2048]{1,0:T(8,128)(2,1)}, u32[]{:S(2)}, u32[]{:S(2)}) collective-permute-start(bf16[128,2048]{1,0:T(8,128)(2,1)} %fusion.31), channel_id=1, source_target_pairs={{0,1},{1,0},{2,3},{3,2},{4,5},{5,4},{6,7},{7,6},{8,9},{9,8},{10,11... | collective-permute-start | bytes 1572872 | tf_op jit(solution)/shard_map/ppermute | solution.py:29
  765.1 6.3 copy-start.11
Sparse Core Ops, SparseCore 0:
  10.8 391.8 all-gather.2
  500.2 261.9 all-reduce.5
where the time goes:
time: 786 us; the launch traced here: 784 us
  waiting for transfers between devices  586 us (75%)
  local copies, waits for them, and re-layouts  82.5 us (10%)
  other arithmetic  53.4 us (7%)
  matrix products  29.2 us (4%)
  starting transfers between devices  18.2 us (2%)
  between operations  14.4 us (2%)
    all_gather x1, waiting for transfers between devices, on_device(): lax.all_gather(summary, ('seq', 'outer'), axis=0, tiled=True)  355 us
    unnamed x3, waiting for transfers between devices  227 us
  transfers between devices with their start and end apart: 10, of which 3 were waited for; matrix products, arithmetic and copies ran while one was open for 7% of the time, Pallas kernels for 0%

commit v1 on v0

v1 whole, which is shorter than its diff:
```python
import functools

import jax
import jax.numpy as jnp
from jax import lax
from jax.experimental import pallas as pl
from jax.experimental.pallas import tpu as pltpu
from jax.sharding import PartitionSpec as P

HEADS = 8
HEAD = 128
LEAF = 128
SPANS = 256
STEPS = 8
PLANE = 32
GROUP = 8
POST_LAG = 2
JOIN_LAG = 4
SCALE = HEAD**-0.5
LOG2E = 1.4426950408889634
MESH = pl.DeviceIdType.MESH
BF16 = jnp.bfloat16
F32 = jnp.float32

SENDS = 11
(S_TILE, S_RIM, S_PAIR, S_QUAD, S_FWD, S_SUM, S_RGRAD, S_PGRAD, S_QGRAD, S_SGRAD, S_BACK) = range(SENDS)
RECVS = 9
(R_RIM, R_PAIR, R_QUAD, R_FWD, R_SUM, R_RGRAD, R_PGRAD, R_QGRAD, R_SGRAD) = range(RECVS)


def dot(a, b, contract):
    return lax.dot_general(a, b, ((contract[:1], contract[1:]), ((), ())), preferred_element_type=F32)


def kernel(
    q, k, v, cot, att, gq, gk, gv, sg,
    tiles_in, sums, rim, pairs, pairs_in, quads, quads_in,
    rgrad, rgrad_in, pgrad, pgrad_in, qkeep, qgrad, qgrad_in,
    sgrad, sgrad_in, stage, back, back_in,
    send, recv, plane_recv,
):
    seq, outer = lax.axis_index("seq"), lax.axis_index("outer")
    x, ylo, z = lax.div(seq, 16), lax.rem(lax.div(seq, 8), 2), lax.rem(seq, 8)
    yhi, core = lax.div(outer, 2), lax.rem(outer, 2)
    span = seq * 4 + outer
    member = z * 4 + ylo * 2 + yhi
    group = x * 2 + core

    def of_span(s):
        return (lax.div(s, 4), lax.rem(s, 4))

    def of_member(m):
        mz, mylo, myhi = lax.div(m, 4), lax.rem(lax.div(m, 2), 2), lax.rem(m, 2)
        return ((x * 2 + mylo) * 8 + mz, myhi * 2 + core)

    def of_group(g):
        gx, gcore = lax.div(g, 2), lax.rem(g, 2)
        return ((gx * 2 + ylo) * 8 + z, yhi * 2 + gcore)

    following = of_span(lax.rem(span + 1, SPANS))
    previous = of_span(lax.rem(span + SPANS - 1, SPANS))
    partner = (seq, yhi * 2 + 1 - core)
    sibling = (seq, (1 - yhi) * 2 + core)

    def post(src, dst, s, r, device):
        pltpu.make_async_remote_copy(
            src_ref=src, dst_ref=dst, send_sem=send.at[s], recv_sem=r, device_id=device, device_id_type=MESH
        ).start()

    def arrived(ref, sem):
        pltpu.make_async_copy(ref, ref, sem).wait()

    barrier = pltpu.get_barrier_semaphore()

    def greet(device):
        pl.semaphore_signal(barrier, inc=1, device_id=device, device_id_type=MESH)

    def greet_plane(d, carry):
        greet(of_member(lax.rem(member + d, PLANE)))
        return carry

    lax.fori_loop(1, PLANE, greet_plane, 0)
    for d in range(1, GROUP):
        greet(of_group(lax.rem(group + d, GROUP)))
    greet(following)
    greet(previous)

    def grid(rows, cols):
        return (
            lax.broadcasted_iota(jnp.int32, (rows, cols), 0),
            lax.broadcasted_iota(jnp.int32, (rows, cols), 1),
        )

    row, col = grid(128, 256)
    halve = jnp.where((col >> 1) == row, 0.5, 0.0).astype(BF16)
    row, col = grid(64, 128)
    halve_again = jnp.where((col >> 1) == row, 0.5, 0.0).astype(BF16)
    row, col = grid(256, 256)
    turn = jnp.where(col == ((row & 15) * 16 + (row >> 4)), 1.0, 0.0).astype(BF16)

    chunks = []
    for kv, ref in enumerate((k, v)):
        whole = ref[...]
        pair_rows = dot(halve, whole, (1, 0)).astype(BF16)
        quad_rows = dot(halve_again, pair_rows, (1, 0)).astype(BF16)
        mean = jnp.sum(whole.astype(F32), axis=0, keepdims=True) * (1.0 / 256)
        chunks += [mean[:, h * HEAD:(h + 1) * HEAD] for h in range(HEADS)]
        for t in range(STEPS):
            pairs[t, kv] = pair_rows[:, t * HEAD:(t + 1) * HEAD]
            quads[t, kv] = quad_rows[:, t * HEAD:(t + 1) * HEAD]
    tiles_in[member] = jnp.concatenate(chunks, axis=0).astype(BF16)

    pl.semaphore_wait(barrier, PLANE - 1 + GROUP - 1 + 2)

    def send_tile(d, carry):
        post(tiles_in.at[member], tiles_in.at[member], S_TILE, plane_recv.at[0], of_member(lax.rem(member + d, PLANE)))
        return carry

    lax.fori_loop(1, PLANE, send_tile, 0)

    def send_step(t, carry):
        cols = pl.ds(pl.multiple_of(t * HEAD, HEAD), HEAD)
        post(quads.at[t], quads_in.at[t, 0], S_QUAD, recv.at[R_QUAD, t], sibling)
        for kv, ref in enumerate((k, v)):
            post(ref.at[pl.ds(LEAF, LEAF), cols], rim.at[t, kv], S_RIM, recv.at[R_RIM, t], following)
            post(ref.at[pl.ds(0, LEAF), cols], rim.at[t, 2 + kv], S_RIM, recv.at[R_RIM, t], previous)
        post(pairs.at[t], pairs_in.at[t], S_PAIR, recv.at[R_PAIR, t], partner)
        return carry

    lax.fori_loop(0, STEPS, send_step, 0)

    arrived(tiles_in.at[pl.ds(0, PLANE - 1)], plane_recv.at[0])
    for part in range(2):
        turned = dot(turn, tiles_in[part * 16:(part + 1) * 16].reshape(256, HEAD), (1, 0)).astype(BF16)
        for t in range(STEPS):
            for kv in range(2):
                at = (kv * 8 + t) * 16
                sums[t, group, kv * 32 + part * 16:kv * 32 + (part + 1) * 16, :] = turned[at:at + 16]

    def send_sums(t, carry):
        for d in range(1, GROUP):
            post(
                sums.at[t, group], sums.at[t, group], S_SUM, recv.at[R_SUM, t],
                of_group(lax.rem(group + d, GROUP)),
            )
        return carry

    lax.fori_loop(0, STEPS, send_sums, 0)

    def forward_quads(t):
        arrived(quads_in.at[t, 0], recv.at[R_QUAD, t])
        post(quads_in.at[t, 0], quads_in.at[t, 1], S_FWD, recv.at[R_FWD, t], partner)

    forward_quads(0)

    row, col = grid(256, 256)
    covered = ((row >> 6) == x) & (((row & 31) >> 1) == z * 2 + ylo)
    row, col = grid(128, 256)
    absent = ((col < LEAF) & (span == 0)) | ((col >= LEAF) & (span == SPANS - 1))

    def compute(t):
        @pl.when(t + 1 < STEPS)
        def _():
            forward_quads(t + 1)

        arrived(rim.at[t], recv.at[R_RIM, t])
        arrived(pairs_in.at[t], recv.at[R_PAIR, t])
        arrived(quads_in.at[t, 1], recv.at[R_FWD, t])
        arrived(sums.at[t, pl.ds(0, GROUP - 1)], recv.at[R_SUM, t])
        cols = pl.ds(pl.multiple_of(t * HEAD, HEAD), HEAD)
        qh, ch = q[:, cols], cot[:, cols]

        def rows_of(kv, ref):
            return jnp.concatenate(
                [
                    ref[:, cols],
                    pairs_in[t, kv],
                    quads_in[t, 0, kv],
                    quads_in[t, 1, kv],
                    sums[t, :, kv * 32:(kv + 1) * 32, :].reshape(SPANS, HEAD),
                ],
                axis=0,
            )

        def against(main, left, right, other):
            at_rim = jnp.concatenate(
                [dot(left, other[:LEAF], (1, 1)), dot(right, other[LEAF:], (1, 1))], axis=1
            )
            return jnp.concatenate([dot(main, other, (1, 1)), at_rim], axis=0)

        def gathered(main, left, right, weights):
            total = dot(main, weights[:768], (0, 0))
            at_rim = jnp.concatenate(
                [dot(left, weights[768:, :LEAF], (0, 0)), dot(right, weights[768:, LEAF:], (0, 0))], axis=1
            )
            return (total + at_rim).T

        keys, values = rows_of(0, k), rows_of(1, v)
        key_l, value_l, key_r, value_r = rim[t, 0], rim[t, 1], rim[t, 2], rim[t, 3]
        scores = against(keys, key_l, key_r, qh)
        scores = jnp.concatenate(
            [
                scores[:512],
                jnp.where(covered, -1e30, scores[512:768]),
                jnp.where(absent, -1e30, scores[768:]),
            ],
            axis=0,
        )
        highest = jnp.max(scores, axis=0, keepdims=True)
        weights = jnp.exp2((scores - highest) * (SCALE * LOG2E))
        probs = weights * (1.0 / jnp.sum(weights, axis=0, keepdims=True))
        probs_low = probs.astype(BF16)
        dprobs = against(values, value_l, value_r, ch)
        centre = jnp.sum(probs * dprobs, axis=0, keepdims=True)
        dscores = (probs * (dprobs - centre)).astype(BF16)

        att[:, cols] = gathered(values, value_l, value_r, probs_low).astype(BF16)
        gq[:, cols] = gathered(keys, key_l, key_r, dscores) * SCALE

        for kv, (low, other, out, factor) in enumerate(((dscores, qh, gk, SCALE), (probs_low, ch, gv, 1.0))):
            main = dot(low[:768], other, (1, 0)) * factor
            out[:, cols] = main[:256]
            pgrad[t, kv, 0:128, :] = main[256:384].astype(BF16)
            qkeep[t, kv] = main[384:448]
            pgrad[t, kv, 128:192, :] = main[448:512].astype(BF16)
            sgrad[t, :, kv * 32:(kv + 1) * 32, :] = main[512:].astype(BF16).reshape(GROUP, 32, HEAD)
            rgrad[t, kv] = (dot(low[768:, :LEAF], other[:LEAF], (1, 0)) * factor).astype(BF16)
            rgrad[t, 2 + kv] = (dot(low[768:, LEAF:], other[LEAF:], (1, 0)) * factor).astype(BF16)

        post(pgrad.at[t], pgrad_in.at[t], S_PGRAD, recv.at[R_PGRAD, t], partner)
        two = pl.ds(0, 2)
        other_two = pl.ds(2, 2)
        post(rgrad.at[t, two], rgrad_in.at[t, other_two], S_RGRAD, recv.at[R_RGRAD, t], previous)
        post(rgrad.at[t, other_two], rgrad_in.at[t, two], S_RGRAD, recv.at[R_RGRAD, t], following)
        for d in range(1, GROUP):
            there = lax.rem(group + d, GROUP)
            post(sgrad.at[t, there], sgrad_in.at[t, group], S_SGRAD, recv.at[R_SGRAD, t], of_group(there))
        sgrad_in[t, group] = sgrad[t, group]

    def reduce(t):
        arrived(pgrad_in.at[t], recv.at[R_PGRAD, t])
        qgrad[t] = (qkeep[t] + pgrad_in[t, :, 128:192, :].astype(F32)).astype(BF16)
        post(qgrad.at[t], qgrad_in.at[t], S_QGRAD, recv.at[R_QGRAD, t], sibling)
        arrived(sgrad_in.at[t, pl.ds(0, GROUP - 1)], recv.at[R_SGRAD, t])
        total = sgrad_in[t, 0].astype(F32)
        for g in range(1, GROUP):
            total = total + sgrad_in[t, g].astype(F32)
        total = total.astype(BF16)
        for kv in range(2):
            for part in range(2):
                at = kv * 32 + part * 16
                stage[part, kv * 8 + t] = total[at:at + 16]

    row, col = grid(256, 128)
    double = jnp.where((row >> 1) == col, 0.5, 0.0).astype(BF16)
    row, col = grid(256, 64)
    double_twice = jnp.where((row >> 2) == col, 0.25, 0.0).astype(BF16)

    def join(t):
        arrived(rgrad_in.at[t], recv.at[R_RGRAD, t])
        arrived(qgrad_in.at[t], recv.at[R_QGRAD, t])
        cols = pl.ds(pl.multiple_of(t * HEAD, HEAD), HEAD)
        for kv, out in enumerate((gk, gv)):
            ends = jnp.concatenate([rgrad_in[t, kv], rgrad_in[t, 2 + kv]], axis=0).astype(F32)
            coarse = dot(double, pgrad_in[t, kv, 0:128, :], (1, 0)) + dot(double_twice, qgrad_in[t, kv], (1, 0))
            out[:, cols] = out[:, cols] + ends + coarse

    def step(t, carry):
        compute(t)

        @pl.when(t >= POST_LAG)
        def _():
            reduce(t - POST_LAG)

        @pl.when(t >= JOIN_LAG)
        def _():
            join(t - JOIN_LAG)

        return carry

    def repeat(f):
        def body(t, carry):
            f(t)
            return carry

        return body

    lax.fori_loop(0, STEPS, step, 0)
    lax.fori_loop(STEPS - POST_LAG, STEPS, repeat(reduce), 0)

    for part in range(2):
        turned = dot(turn, stage[part].reshape(256, HEAD), (1, 0)).astype(BF16)
        back[part * 16:(part + 1) * 16] = turned.reshape(16, 16, HEAD)

    back_in[member] = back[member]

    def send_back(d, carry):
        there = lax.rem(member + d, PLANE)
        post(back.at[there], back_in.at[member], S_BACK, plane_recv.at[1], of_member(there))
        return carry

    lax.fori_loop(1, PLANE, send_back, 0)
    lax.fori_loop(STEPS - JOIN_LAG, STEPS, repeat(join), 0)

    arrived(back_in.at[pl.ds(0, PLANE - 1)], plane_recv.at[1])
    total = back_in[0].astype(F32)
    for m in range(1, PLANE):
        total = total + back_in[m].astype(F32)
    for kv, out in enumerate((gk, gv)):
        for h in range(HEADS):
            row = total[kv * 8 + h:kv * 8 + h + 1]
            sg[:, (kv * 8 + h) * HEAD:(kv * 8 + h + 1) * HEAD] = row
            out[:, h * HEAD:(h + 1) * HEAD] = out[:, h * HEAD:(h + 1) * HEAD] + row * (1.0 / 256)

    arrived(tiles_in.at[pl.ds(0, PLANE - 1)], send.at[S_TILE])
    arrived(rim, send.at[S_RIM])
    arrived(pairs, send.at[S_PAIR])
    arrived(quads, send.at[S_QUAD])
    arrived(quads, send.at[S_FWD])
    arrived(sums.at[:, pl.ds(0, GROUP - 1)], send.at[S_SUM])
    arrived(rgrad, send.at[S_RGRAD])
    arrived(pgrad, send.at[S_PGRAD])
    arrived(qgrad, send.at[S_QGRAD])
    arrived(sgrad.at[:, pl.ds(0, GROUP - 1)], send.at[S_SGRAD])
    arrived(back.at[pl.ds(0, PLANE - 1)], send.at[S_BACK])


def on_device(queries, keys, values, cotangent):
    rows, width = queries.shape
    in_vmem = pl.BlockSpec(memory_space=pltpu.VMEM)
    block = (STEPS, 4, LEAF, HEAD)
    return pl.pallas_call(
        kernel,
        out_shape=(
            jax.ShapeDtypeStruct((rows, width), BF16),
            jax.ShapeDtypeStruct((rows, width), F32),
            jax.ShapeDtypeStruct((rows, width), F32),
            jax.ShapeDtypeStruct((rows, width), F32),
            jax.ShapeDtypeStruct((1, 2 * width), F32),
        ),
        in_specs=[in_vmem] * 4,
        out_specs=(in_vmem,) * 5,
        scratch_shapes=[
            pltpu.VMEM((PLANE, 16, HEAD), BF16),
            pltpu.VMEM((STEPS, GROUP, 64, HEAD), BF16),
            pltpu.VMEM(block, BF16),
            pltpu.VMEM((STEPS, 2, 128, HEAD), BF16),
            pltpu.VMEM((STEPS, 2, 128, HEAD), BF16),
            pltpu.VMEM((STEPS, 2, 64, HEAD), BF16),
            pltpu.VMEM((STEPS, 2, 2, 64, HEAD), BF16),
            pltpu.VMEM(block, BF16),
            pltpu.VMEM(block, BF16),
            pltpu.VMEM((STEPS, 2, 192, HEAD), BF16),
            pltpu.VMEM((STEPS, 2, 192, HEAD), BF16),
            pltpu.VMEM((STEPS, 2, 64, HEAD), F32),
            pltpu.VMEM((STEPS, 2, 64, HEAD), BF16),
            pltpu.VMEM((STEPS, 2, 64, HEAD), BF16),
            pltpu.VMEM((STEPS, GROUP, 64, HEAD), BF16),
            pltpu.VMEM((STEPS, GROUP, 64, HEAD), BF16),
            pltpu.VMEM((2, 16, 16, HEAD), BF16),
            pltpu.VMEM((PLANE, 16, HEAD), BF16),
            pltpu.VMEM((PLANE, 16, HEAD), BF16),
            pltpu.SemaphoreType.DMA((SENDS,)),
            pltpu.SemaphoreType.DMA((RECVS, STEPS)),
            pltpu.SemaphoreType.DMA((2,)),
        ],
        compiler_params=pltpu.CompilerParams(
            collective_id=0, has_side_effects=True, vmem_limit_bytes=48 * 2**20
        ),
        name="attend",
    )(queries, keys, values, cotangent)


def solution(mesh):
    spec = P(("seq", "outer"), None)
    return jax.shard_map(
        on_device, mesh=mesh, in_specs=(spec,) * 4, out_specs=(spec,) * 5, check_vma=False
    )
```

time: 786 us -> 67.6 us (0.09)
  waiting for transfers between devices: 586 us -> 0 us
  local copies, waits for them, and re-layouts: 82.5 us -> 8.46 us
  Pallas kernels: 0 us -> 58.2 us
  other arithmetic: 53.4 us -> 0 us
  matrix products: 29.2 us -> 0 us
  starting transfers between devices: 18.2 us -> 0 us
  between operations: 14.4 us -> 0.65 us
    all_gather x1 -> x0, waiting for transfers between devices: 355 us -> none  [on_device(): lax.all_gather(summary, ('seq', 'outer'), axis=0, tiled=True)]
    unnamed x3 -> x0, waiting for transfers between devices: 227 us -> none
    pallas_call x0 -> x1, Pallas kernels: none -> 58.2 us  [on_device(): pl.pallas_call(kernel, out_shape=(jax.ShapeDtypeStruct((rows, width), BF1...]
    dot_general x5 -> x0, matrix products: 21.2 us -> none  [the longest x1 6.26 us: attend(): jnp.einsum('bhqk,bkhe->bqhe', probs_low, values_h, preferred_element_type...]
    mul x5 -> x0, local copies, waits for them, and re-layouts: 20.1 us -> none  [the longest x1 8.05 us: attend(): jnp.einsum('bhqk,bqhe->bkhe', dscores, queries_h, preferred_element_type=...]
    reshape x4 -> x0, local copies, waits for them, and re-layouts: 19.8 us -> none  [the longest x1 8.26 us: attend(): grad_k.reshape(leaf_count, set_size, feat_width)]
    ppermute x8 -> x0, starting transfers between devices: 18.1 us -> none  [the longest x4 7.69 us: swapped(): return lax.ppermute(value, axis, pairs)]
    convert_element_type x9 -> x0, other arithmetic: 17.5 us -> none  [the longest x1 6.61 us: attend(): dscores = (probs * (dprobs - centre)).astype(jnp.bfloat16)]
  transfers between devices with their start and end apart: 10 -> 0, of which waited for: 3 -> 0; matrix products, arithmetic and copies ran while one was open for 7% -> 0% of each run, Pallas kernels for 0% -> 0%
where the time goes in v1:
time: 67.6 us; the launch traced here: 67.3 us
  Pallas kernels  58.2 us (86%)
  local copies, waits for them, and re-layouts  8.46 us (13%)
    pallas_call x1, Pallas kernels, on_device(): pl.pallas_call(kernel, out_shape=(jax.ShapeDtypeStruct((rows, width), BF1...  58.2 us
    unnamed x13, local copies, waits for them, and re-layouts  8.46 us

profile of v1, /device:TPU:1, one launch (start us, length us, event | category | flops | bytes accessed | tf_op | source)
XLA Modules:
  0.0 67.3 jit_solution(304254040136461110)
XLA Ops:
  0.6 0.0 copy-start
  0.6 1.0 %copy-done = bf16[256,1024]{1,0:T(8,128)(2,1)S(1)} copy-done((bf16[256,1024]{1,0:T(8,128)(2,1)S(1)}, bf16[256,1024]{1,0:T(8,128)(2,1)}, u32[]{:S(2)}) %copy-start) | copy-done | bytes 524312
  1.7 0.0 copy-start.1
  1.7 1.0 %copy-done.1 = bf16[256,1024]{1,0:T(8,128)(2,1)S(1)} copy-done((bf16[256,1024]{1,0:T(8,128)(2,1)S(1)}, bf16[256,1024]{1,0:T(8,128)(2,1)}, u32[]{:S(2)}) %copy-start.1) | copy-done | bytes 524312
  2.7 0.0 copy-start.2
  2.7 1.0 %copy-done.2 = bf16[256,1024]{1,0:T(8,128)(2,1)S(1)} copy-done((bf16[256,1024]{1,0:T(8,128)(2,1)S(1)}, bf16[256,1024]{1,0:T(8,128)(2,1)}, u32[]{:S(2)}) %copy-start.2) | copy-done | bytes 524312
  3.8 0.0 copy-start.3
  3.8 1.0 %copy-done.3 = bf16[256,1024]{1,0:T(8,128)(2,1)S(1)} copy-done((bf16[256,1024]{1,0:T(8,128)(2,1)S(1)}, bf16[256,1024]{1,0:T(8,128)(2,1)}, u32[]{:S(2)}) %copy-start.3) | copy-done | bytes 524312
  4.8 58.2 %attend.1 = (bf16[256,1024]{1,0:T(8,128)(2,1)S(1)}, f32[256,1024]{1,0:T(8,128)S(1)}, f32[256,1024]{1,0:T(8,128)S(1)}, f32[256,1024]{1,0:T(8,128)S(1)}, f32[1,2048]{1,0:T(1,128)S(1)}) custom-call(bf16[256,1024]{1,0:T(8,128)(2,1)S(1)} %copy-done, bf16[256,1024]{1,0:T(8,128)(2,1)S(1)} %copy-done.1, bf16[256,1024]{1,0:T(8,128)(2,1)S(1)} %copy-done.2, ...), custom_call_target="tpu_custom_call" | custom-call | tf_op jit(solution)/shard_map/attend/pallas_call | solution.py:332
  63.0 0.8 %copy.14 = bf16[256,1024]{1,0:T(8,128)(2,1)} copy(bf16[256,1024]{1,0:T(8,128)(2,1)S(1)} %get-tuple-element.10) | data formatting | bytes 1048576
  63.8 1.0 %copy.15 = f32[256,1024]{1,0:T(8,128)} copy(f32[256,1024]{1,0:T(8,128)S(1)} %get-tuple-element.11) | data formatting | bytes 2097152
  64.8 1.0 %copy.16 = f32[256,1024]{1,0:T(8,128)} copy(f32[256,1024]{1,0:T(8,128)S(1)} %get-tuple-element.12) | data formatting | bytes 2097152
  65.7 1.0 %copy.17 = f32[256,1024]{1,0:T(8,128)} copy(f32[256,1024]{1,0:T(8,128)S(1)} %get-tuple-element.13) | data formatting | bytes 2097152
  66.7 0.6 copy.18
Async XLA Ops:
  0.6 1.0 %copy-start = (bf16[256,1024]{1,0:T(8,128)(2,1)S(1)}, bf16[256,1024]{1,0:T(8,128)(2,1)}, u32[]{:S(2)}) copy-start(bf16[256,1024]{1,0:T(8,128)(2,1)} %q.1) | copy-start | bytes 1572868
  1.7 1.0 %copy-start.1 = (bf16[256,1024]{1,0:T(8,128)(2,1)S(1)}, bf16[256,1024]{1,0:T(8,128)(2,1)}, u32[]{:S(2)}) copy-start(bf16[256,1024]{1,0:T(8,128)(2,1)} %k.1) | copy-start | bytes 1572868
  2.7 1.0 %copy-start.2 = (bf16[256,1024]{1,0:T(8,128)(2,1)S(1)}, bf16[256,1024]{1,0:T(8,128)(2,1)}, u32[]{:S(2)}) copy-start(bf16[256,1024]{1,0:T(8,128)(2,1)} %v.1) | copy-start | bytes 1572868
  3.8 1.0 %copy-start.3 = (bf16[256,1024]{1,0:T(8,128)(2,1)S(1)}, bf16[256,1024]{1,0:T(8,128)(2,1)}, u32[]{:S(2)}) copy-start(bf16[256,1024]{1,0:T(8,128)(2,1)} %cot.1) | copy-start | bytes 1572868

commit v2 on v1

v2 whole, which is shorter than its diff:
```python
import functools

import jax
import jax.numpy as jnp
from jax import lax
from jax.experimental import pallas as pl
from jax.experimental.pallas import tpu as pltpu
from jax.sharding import PartitionSpec as P

HEADS = 8
HEAD = 128
LEAF = 128
SPANS = 256
STEPS = 8
PLANE = 32
ZS, YS, XS = 8, 4, 4
GROUP = 2 * XS
HALF_LAG = 2
POST_LAG = 5
SCALE = HEAD**-0.5
LOG2E = 1.4426950408889634
MESH = pl.DeviceIdType.MESH
BF16 = jnp.bfloat16
F32 = jnp.float32

(
    S_TILE, S_RIM, S_PAIR, S_QUAD, S_QFWD, S_SUM, S_RGRAD, S_PGRAD, S_QGRAD, S_SGRAD, S_BACK,
) = range(11)
R_RIM, R_PAIR, R_QUAD, R_QFWD, R_SUM, R_RGRAD, R_PGRAD, R_QGRAD, R_SGRAD = range(9)


def dot(a, b, contract):
    return lax.dot_general(a, b, ((contract[:1], contract[1:]), ((), ())), preferred_element_type=F32)


def kernel(
    q_in, k_in, v_in, cot_in, att_out, gq_out, gk_out, gv_out, sg_out,
    q, k, v, cot, att, gq, gk, gv, sg,
    tiles_in, sums, rim, pairs, pairs_in, quads, quads_in,
    rgrad, rgrad_in, pgrad, pgrad_in, qkeep, qgrad, qgrad_in,
    sgrad, sgrad_in, probs_kept, dscores_kept, stage, back, back_in,
    send, recv, plane_recv, load, store,
):
    seq, outer = lax.axis_index("seq"), lax.axis_index("outer")
    x, ylo, z = lax.div(seq, 16), lax.rem(lax.div(seq, 8), 2), lax.rem(seq, 8)
    yhi, core = lax.div(outer, 2), lax.rem(outer, 2)
    span = seq * 4 + outer
    y = ylo * 2 + yhi
    member = z * 4 + y

    def at(x, y, z):
        return ((x * 2 + lax.div(y, 2)) * 8 + z, lax.rem(y, 2) * 2 + core)

    def of_span(s):
        return (lax.div(s, 4), lax.rem(s, 4))

    following = of_span(lax.rem(span + 1, SPANS))
    previous = of_span(lax.rem(span + SPANS - 1, SPANS))
    partner = (seq, yhi * 2 + 1 - core)
    sibling = (seq, (1 - yhi) * 2 + core)
    plane = [
        (lax.rem(z + dz, ZS) * YS + lax.rem(y + dy, YS), at(x, lax.rem(y + dy, YS), lax.rem(z + dz, ZS)))
        for dz in (4, 3, 5, 2, 6, 1, 7, 0)
        for dy in (2, 1, 3, 0)
        if dz or dy
    ]
    group = core * XS + x
    mates = []
    for dx, dcore in ((2, 0), (2, 1), (1, 0), (3, 0), (1, 1), (3, 1), (0, 1)):
        mx, mcore = lax.rem(x + dx, XS), lax.rem(core + dcore, 2)
        mates.append((mcore * XS + mx, ((mx * 2 + ylo) * 8 + z, yhi * 2 + mcore)))

    loads = [
        pltpu.make_async_copy(src, dst, load.at[i])
        for i, (src, dst) in enumerate(((k_in, k), (v_in, v), (q_in, q), (cot_in, cot)))
    ]
    for copy in loads:
        copy.start()

    def post(src, dst, s, r, device):
        pltpu.make_async_remote_copy(
            src_ref=src, dst_ref=dst, send_sem=send.at[s], recv_sem=r, device_id=device, device_id_type=MESH
        ).start()

    def arrived(ref, sem):
        pltpu.make_async_copy(ref, ref, sem).wait()

    barrier = pltpu.get_barrier_semaphore()

    def greet(device):
        pl.semaphore_signal(barrier, inc=1, device_id=device, device_id_type=MESH)

    for _, device in plane + mates:
        greet(device)
    greet(following)
    greet(previous)

    def grid(rows, cols):
        return (
            lax.broadcasted_iota(jnp.int32, (rows, cols), 0),
            lax.broadcasted_iota(jnp.int32, (rows, cols), 1),
        )

    row, col = grid(128, 256)
    halve = jnp.where((col >> 1) == row, 0.5, 0.0).astype(BF16)
    row, col = grid(64, 128)
    halve_again = jnp.where((col >> 1) == row, 0.5, 0.0).astype(BF16)
    row, col = grid(256, 256)
    turn = jnp.where(col == ((row & 15) * 16 + (row >> 4)), 1.0, 0.0).astype(BF16)

    loads[0].wait()
    loads[1].wait()
    chunks = []
    for kv, ref in enumerate((k, v)):
        whole = ref[...]
        pair_rows = dot(halve, whole, (1, 0)).astype(BF16)
        quad_rows = dot(halve_again, pair_rows, (1, 0)).astype(BF16)
        mean = jnp.sum(whole.astype(F32), axis=0, keepdims=True) * (1.0 / 256)
        chunks += [mean[:, h * HEAD:(h + 1) * HEAD] for h in range(HEADS)]
        for t in range(STEPS):
            pairs[t, kv] = pair_rows[:, t * HEAD:(t + 1) * HEAD]
            quads[t, kv] = quad_rows[:, t * HEAD:(t + 1) * HEAD]
    tiles_in[member] = jnp.concatenate(chunks, axis=0).astype(BF16)

    pl.semaphore_wait(barrier, len(plane) + len(mates) + 2)

    for _, device in plane:
        post(tiles_in.at[member], tiles_in.at[member], S_TILE, plane_recv.at[0], device)

    def send_step(t, carry):
        cols = pl.ds(pl.multiple_of(t * HEAD, HEAD), HEAD)
        post(quads.at[t], quads_in.at[t, 0], S_QUAD, recv.at[R_QUAD, t], sibling)
        for kv, ref in enumerate((k_in, v_in)):
            post(ref.at[pl.ds(LEAF, LEAF), cols], rim.at[t, kv], S_RIM, recv.at[R_RIM, t], following)
            post(ref.at[pl.ds(0, LEAF), cols], rim.at[t, 2 + kv], S_RIM, recv.at[R_RIM, t], previous)
        post(pairs.at[t], pairs_in.at[t], S_PAIR, recv.at[R_PAIR, t], partner)
        return carry

    lax.fori_loop(0, STEPS, send_step, 0)

    arrived(tiles_in.at[pl.ds(0, PLANE - 1)], plane_recv.at[0])
    for part in range(2):
        turned = dot(turn, tiles_in[part * 16:(part + 1) * 16].reshape(256, HEAD), (1, 0)).astype(BF16)
        for t in range(STEPS):
            for kv in range(2):
                first = (kv * 8 + t) * 16
                sums[t, group, kv * 32 + part * 16:kv * 32 + (part + 1) * 16, :] = turned[first:first + 16]

    def send_sums(t, carry):
        for _, device in mates:
            post(sums.at[t, group], sums.at[t, group], S_SUM, recv.at[R_SUM, t], device)
        return carry

    lax.fori_loop(0, STEPS, send_sums, 0)

    def forward(t):
        arrived(quads_in.at[t, 0], recv.at[R_QUAD, t])
        post(quads_in.at[t, 0], quads_in.at[t, 1], S_QFWD, recv.at[R_QFWD, t], partner)

    forward(0)
    loads[2].wait()
    loads[3].wait()

    row, col = grid(256, 256)
    covered = (((row >> 5) & 3) == x) & (((row & 31) >> 1) == z * 2 + ylo)
    row, col = grid(128, 256)
    absent = ((col < LEAF) & (span == 0)) | ((col >= LEAF) & (span == SPANS - 1))

    def columns(t):
        return pl.ds(pl.multiple_of(t * HEAD, HEAD), HEAD)

    def rows_of(t, kv, ref):
        return jnp.concatenate(
            [
                ref[:, columns(t)],
                pairs_in[t, kv],
                quads_in[t, 0, kv],
                quads_in[t, 1, kv],
                sums[t, :, kv * 32:(kv + 1) * 32, :].reshape(SPANS, HEAD),
            ],
            axis=0,
        )

    def compute(t):
        @pl.when(t + 1 < STEPS)
        def _():
            forward(t + 1)

        arrived(rim.at[t], recv.at[R_RIM, t])
        arrived(pairs_in.at[t], recv.at[R_PAIR, t])
        arrived(quads_in.at[t, 1], recv.at[R_QFWD, t])
        arrived(sums.at[t, pl.ds(0, GROUP - 1)], recv.at[R_SUM, t])
        cols = columns(t)
        qh, ch = q[:, cols], cot[:, cols]

        def against(main, left, right, other):
            at_rim = jnp.concatenate(
                [dot(left, other[:LEAF], (1, 1)), dot(right, other[LEAF:], (1, 1))], axis=1
            )
            return jnp.concatenate([dot(main, other, (1, 1)), at_rim], axis=0)

        keys, values = rows_of(t, 0, k), rows_of(t, 1, v)
        key_l, value_l, key_r, value_r = rim[t, 0], rim[t, 1], rim[t, 2], rim[t, 3]
        scores = against(keys, key_l, key_r, qh)
        scores = jnp.concatenate(
            [
                scores[:512],
                jnp.where(covered, -1e30, scores[512:768]),
                jnp.where(absent, -1e30, scores[768:]),
            ],
            axis=0,
        )
        highest = jnp.max(scores, axis=0, keepdims=True)
        weights = jnp.exp2((scores - highest) * (SCALE * LOG2E))
        probs = weights * (1.0 / jnp.sum(weights, axis=0, keepdims=True))
        probs_low = probs.astype(BF16)
        dprobs = against(values, value_l, value_r, ch)
        centre = jnp.sum(probs * dprobs, axis=0, keepdims=True)
        dscores = (probs * (dprobs - centre)).astype(BF16)

        probs_kept[t] = probs_low
        dscores_kept[t] = dscores

        sides = ((dscores, qh, SCALE), (probs_low, ch, 1.0))
        for kv, (low, other, factor) in enumerate(sides):
            far = (dot(low[512:768], other, (1, 0)) * factor).astype(BF16)
            sgrad[t, :, kv * 32:(kv + 1) * 32, :] = far.reshape(GROUP, 32, HEAD)
        for there, device in mates:
            post(sgrad.at[t, there], sgrad_in.at[t, group], S_SGRAD, recv.at[R_SGRAD, t], device)
        sgrad_in[t, group] = sgrad[t, group]

        for kv, (low, other, factor) in enumerate(sides):
            rgrad[t, kv] = (dot(low[768:, :LEAF], other[:LEAF], (1, 0)) * factor).astype(BF16)
            rgrad[t, 2 + kv] = (dot(low[768:, LEAF:], other[LEAF:], (1, 0)) * factor).astype(BF16)
        two, other_two = pl.ds(0, 2), pl.ds(2, 2)
        post(rgrad.at[t, two], rgrad_in.at[t, other_two], S_RGRAD, recv.at[R_RGRAD, t], previous)
        post(rgrad.at[t, other_two], rgrad_in.at[t, two], S_RGRAD, recv.at[R_RGRAD, t], following)

        for kv, (low, other, factor) in enumerate(sides):
            coarse = dot(low[256:512], other, (1, 0)) * factor
            pgrad[t, kv, 0:128, :] = coarse[:128].astype(BF16)
            qkeep[t, kv] = coarse[128:192]
            pgrad[t, kv, 128:192, :] = coarse[192:].astype(BF16)
        post(pgrad.at[t], pgrad_in.at[t], S_PGRAD, recv.at[R_PGRAD, t], partner)

    def gathered(t, kv, ref, weights):
        total = dot(rows_of(t, kv, ref), weights[:768], (0, 0))
        at_rim = jnp.concatenate(
            [
                dot(rim[t, kv], weights[768:, :LEAF], (0, 0)),
                dot(rim[t, 2 + kv], weights[768:, LEAF:], (0, 0)),
            ],
            axis=1,
        )
        return (total + at_rim).T

    def gather(t):
        att[:, columns(t)] = gathered(t, 1, v, probs_kept[t]).astype(BF16)
        gq[:, columns(t)] = gathered(t, 0, k, dscores_kept[t]) * SCALE

    def halves(t):
        arrived(pgrad_in.at[t], recv.at[R_PGRAD, t])
        qgrad[t] = (qkeep[t] + pgrad_in[t, :, 128:192, :].astype(F32)).astype(BF16)
        post(qgrad.at[t], qgrad_in.at[t], S_QGRAD, recv.at[R_QGRAD, t], sibling)

    def reduce(t):
        arrived(sgrad_in.at[t, pl.ds(0, GROUP - 1)], recv.at[R_SGRAD, t])
        total = jnp.sum(sgrad_in[t].astype(F32), axis=0).astype(BF16)
        for kv in range(2):
            for part in range(2):
                first = kv * 32 + part * 16
                stage[part, kv * 8 + t] = total[first:first + 16]

    row, col = grid(256, 128)
    double = jnp.where((row >> 1) == col, 0.5, 0.0).astype(BF16)
    row, col = grid(256, 64)
    double_twice = jnp.where((row >> 2) == col, 0.25, 0.0).astype(BF16)

    def join(t):
        arrived(rgrad_in.at[t], recv.at[R_RGRAD, t])
        arrived(qgrad_in.at[t], recv.at[R_QGRAD, t])
        cols = columns(t)
        sides = ((dscores_kept, q, gk, gk_out, SCALE), (probs_kept, cot, gv, gv_out, 1.0))
        for kv, (low, other, out, out_hbm, factor) in enumerate(sides):
            own = dot(low[t, 0:256, :], other[:, cols], (1, 0)) * factor
            ends = jnp.concatenate([rgrad_in[t, kv], rgrad_in[t, 2 + kv]], axis=0).astype(F32)
            coarse = dot(double, pgrad_in[t, kv, 0:128, :], (1, 0)) + dot(double_twice, qgrad_in[t, kv], (1, 0))
            out[:, cols] = own + ends + coarse
            pltpu.make_async_copy(out.at[:, cols], out_hbm.at[:, cols], store.at[kv]).start()

    def step(t, carry):
        compute(t)

        @pl.when(t >= HALF_LAG)
        def _():
            halves(t - HALF_LAG)

        @pl.when(t >= POST_LAG)
        def _():
            reduce(t - POST_LAG)

        return carry

    def repeat(f):
        def body(t, carry):
            f(t)
            return carry

        return body

    lax.fori_loop(0, STEPS, step, 0)
    lax.fori_loop(STEPS - HALF_LAG, STEPS, repeat(halves), 0)
    lax.fori_loop(STEPS - POST_LAG, STEPS, repeat(reduce), 0)

    for part in range(2):
        turned = dot(turn, stage[part].reshape(256, HEAD), (1, 0)).astype(BF16)
        back[part * 16:(part + 1) * 16] = turned.reshape(16, 16, HEAD)
    for there, device in plane:
        post(back.at[there], back_in.at[member], S_BACK, plane_recv.at[1], device)
    back_in[member] = back[member]

    lax.fori_loop(0, STEPS, repeat(gather), 0)
    stores = [
        pltpu.make_async_copy(src, dst, store.at[2 + i])
        for i, (src, dst) in enumerate(((att, att_out), (gq, gq_out), (sg, sg_out)))
    ]
    stores[0].start()
    stores[1].start()
    lax.fori_loop(0, STEPS, repeat(join), 0)
    arrived(back_in.at[pl.ds(0, PLANE - 1)], plane_recv.at[1])
    total = jnp.sum(back_in[...].astype(F32), axis=0)
    for c in range(2 * HEADS):
        sg[:, c * HEAD:(c + 1) * HEAD] = total[c:c + 1]
    stores[2].start()

    arrived(tiles_in.at[pl.ds(0, PLANE - 1)], send.at[S_TILE])
    arrived(rim, send.at[S_RIM])
    arrived(pairs, send.at[S_PAIR])
    arrived(quads, send.at[S_QUAD])
    arrived(quads, send.at[S_QFWD])
    arrived(sums.at[:, pl.ds(0, GROUP - 1)], send.at[S_SUM])
    arrived(rgrad, send.at[S_RGRAD])
    arrived(pgrad, send.at[S_PGRAD])
    arrived(qgrad, send.at[S_QGRAD])
    arrived(sgrad.at[:, pl.ds(0, GROUP - 1)], send.at[S_SGRAD])
    arrived(back.at[pl.ds(0, PLANE - 1)], send.at[S_BACK])
    arrived(gk, store.at[0])
    arrived(gv, store.at[1])
    for copy in stores:
        copy.wait()


def finish(att, gq, gk, gv, sg, att_out, gq_out, gk_out, gv_out, sg_out, kept, low, row, load, store):
    through = ((sg, row, sg_out), (gk, kept.at[0], gk_out), (gv, kept.at[1], gv_out), (gq, kept.at[2], gq_out), (att, low, att_out))
    loads = [pltpu.make_async_copy(src, via, load.at[i]) for i, (src, via, _) in enumerate(through)]
    stores = [pltpu.make_async_copy(via, dst, store.at[i]) for i, (_, via, dst) in enumerate(through)]
    for copy in loads:
        copy.start()
    width = kept.shape[2]
    for i in range(5):
        loads[i].wait()
        if i in (1, 2):
            kept[i - 1] = kept[i - 1] + row[:, (i - 1) * width:i * width] * (1.0 / 256)
        stores[i].start()
    for copy in stores:
        copy.wait()


def on_device(queries, keys, values, cotangent):
    rows, width = queries.shape
    in_vmem = pl.BlockSpec(memory_space=pltpu.VMEM)
    in_hbm = pl.BlockSpec(memory_space=pltpu.HBM)
    out_shape = (
        jax.ShapeDtypeStruct((rows, width), BF16),
        jax.ShapeDtypeStruct((rows, width), F32),
        jax.ShapeDtypeStruct((rows, width), F32),
        jax.ShapeDtypeStruct((rows, width), F32),
        jax.ShapeDtypeStruct((1, 2 * width), F32),
    )
    block = (STEPS, 4, LEAF, HEAD)
    parts = pl.pallas_call(
        kernel,
        out_shape=out_shape,
        in_specs=[in_hbm] * 4,
        out_specs=(in_hbm,) * 5,
        scratch_shapes=[pltpu.VMEM((rows, width), BF16)] * 5 + [pltpu.VMEM((rows, width), F32)] * 3 + [
            pltpu.VMEM((1, 2 * width), F32),
            pltpu.VMEM((PLANE, 16, HEAD), BF16),
            pltpu.VMEM((STEPS, GROUP, 64, HEAD), BF16),
            pltpu.VMEM(block, BF16),
            pltpu.VMEM((STEPS, 2, 128, HEAD), BF16),
            pltpu.VMEM((STEPS, 2, 128, HEAD), BF16),
            pltpu.VMEM((STEPS, 2, 64, HEAD), BF16),
            pltpu.VMEM((STEPS, 2, 2, 64, HEAD), BF16),
            pltpu.VMEM(block, BF16),
            pltpu.VMEM(block, BF16),
            pltpu.VMEM((STEPS, 2, 192, HEAD), BF16),
            pltpu.VMEM((STEPS, 2, 192, HEAD), BF16),
            pltpu.VMEM((STEPS, 2, 64, HEAD), F32),
            pltpu.VMEM((STEPS, 2, 64, HEAD), BF16),
            pltpu.VMEM((STEPS, 2, 64, HEAD), BF16),
            pltpu.VMEM((STEPS, GROUP, 64, HEAD), BF16),
            pltpu.VMEM((STEPS, GROUP, 64, HEAD), BF16),
            pltpu.VMEM((STEPS, 896, 256), BF16),
            pltpu.VMEM((STEPS, 896, 256), BF16),
            pltpu.VMEM((2, 16, 16, HEAD), BF16),
            pltpu.VMEM((PLANE, 16, HEAD), BF16),
            pltpu.VMEM((PLANE, 16, HEAD), BF16),
            pltpu.SemaphoreType.DMA((11,)),
            pltpu.SemaphoreType.DMA((9, STEPS)),
            pltpu.SemaphoreType.DMA((2,)),
            pltpu.SemaphoreType.DMA((4,)),
            pltpu.SemaphoreType.DMA((5,)),
        ],
        compiler_params=pltpu.CompilerParams(
            collective_id=0, has_side_effects=True, vmem_limit_bytes=62 * 2**20
        ),
        name="attend",
    )(queries, keys, values, cotangent)
    return pl.pallas_call(
        finish,
        out_shape=out_shape,
        in_specs=[in_hbm] * 5,
        out_specs=(in_hbm,) * 5,
        scratch_shapes=[
            pltpu.VMEM((3, rows, width), F32),
            pltpu.VMEM((rows, width), BF16),
            pltpu.VMEM((1, 2 * width), F32),
            pltpu.SemaphoreType.DMA((5,)),
            pltpu.SemaphoreType.DMA((5,)),
        ],
        compiler_params=pltpu.CompilerParams(vmem_limit_bytes=62 * 2**20),
        name="finish",
    )(*parts)


def solution(mesh):
    spec = P(("seq", "outer"), None)
    return jax.shard_map(
        on_device, mesh=mesh, in_specs=(spec,) * 4, out_specs=(spec,) * 5, check_vma=False
    )
```

time: 67.6 us -> 60.6 us (0.90)
  the two profiles are of different devices: /device:TPU:1 before, /device:TPU:25 now
where the time goes in v2:
time: 60.6 us; the launch traced here: 60.5 us
  Pallas kernels  59.8 us (99%)
  between operations  0.64 us (1%)
    pallas_call x1, Pallas kernels, on_device(): pl.pallas_call(kernel, out_shape=out_shape, in_specs=[in_hbm] * 4, out_sp...  56.6 us
    pallas_call x1, Pallas kernels, on_device(): pl.pallas_call(finish, out_shape=out_shape, in_specs=[in_hbm] * 5, out_sp...  3.23 us

profile of v2, /device:TPU:25, one launch (start us, length us, event | category | flops | bytes accessed | tf_op | source)
XLA Modules:
  0.0 60.5 jit_solution(3692262118470220470)
XLA Ops:
  0.6 56.6 %attend.1 = (bf16[256,1024]{1,0:T(8,128)(2,1)}, f32[256,1024]{1,0:T(8,128)}, f32[256,1024]{1,0:T(8,128)}, f32[256,1024]{1,0:T(8,128)}, f32[1,2048]{1,0:T(1,128)}) custom-call(bf16[256,1024]{1,0:T(8,128)(2,1)} %q_in.1, bf16[256,1024]{1,0:T(8,128)(2,1)} %k_in.1, bf16[256,1024]{1,0:T(8,128)(2,1)} %v_in.1, bf16[256,1024]{1,0:T(8,128)(2,1)} %cot_in.1), custom_call_target="tpu_custom_call" | custom-call | tf_op jit(solution)/shard_map/attend/pallas_call | solution.py:381
  57.2 3.2 %finish.1 = (bf16[256,1024]{1,0:T(8,128)(2,1)}, f32[256,1024]{1,0:T(8,128)}, f32[256,1024]{1,0:T(8,128)}, f32[256,1024]{1,0:T(8,128)}, f32[1,2048]{1,0:T(1,128)}) custom-call(bf16[256,1024]{1,0:T(8,128)(2,1)} %get-tuple-element.10.att, f32[256,1024]{1,0:T(8,128)} %get-tuple-element.11.gq, f32[256,1024]{1,0:T(8,128)} %get-tuple-element.12.gk, ...), custom_call_target="tpu_custom_call" | custom-call | tf_op jit(solution)/shard_map/finish/pallas_call | solution.py:420

commit v3 on v2

--- a/solution.py
+++ b/solution.py
@@ -15,6 +15,7 @@
 PLANE = 32
 ZS, YS, XS = 8, 4, 4
 GROUP = 2 * XS
+HOLD = 3
 HALF_LAG = 2
 POST_LAG = 5
 SCALE = HEAD**-0.5
@@ -34,12 +35,13 @@
 
 
 def kernel(
-    q_in, k_in, v_in, cot_in, att_out, gq_out, gk_out, gv_out, sg_out,
-    q, k, v, cot, att, gq, gk, gv, sg,
+    q_in, k_in, v_in, cot_in,
+    att0, att1, gq0, gq1, gq2, gq3, gk0, gk1, gk2, gk3, gv0, gv1, gv2, gv3, sg,
+    q, k, v, cot,
     tiles_in, sums, rim, pairs, pairs_in, quads, quads_in,
     rgrad, rgrad_in, pgrad, pgrad_in, qkeep, qgrad, qgrad_in,
     sgrad, sgrad_in, probs_kept, dscores_kept, stage, back, back_in,
-    send, recv, plane_recv, load, store,
+    send, recv, plane_recv, load,
 ):
     seq, outer = lax.axis_index("seq"), lax.axis_index("outer")
     x, ylo, z = lax.div(seq, 16), lax.rem(lax.div(seq, 8), 2), lax.rem(seq, 8)
@@ -180,6 +182,11 @@
             ],
             axis=0,
         )
+
+    def send_rims(t):
+        two, other_two = pl.ds(0, 2), pl.ds(2, 2)
+        post(rgrad.at[t, two], rgrad_in.at[t, other_two], S_RGRAD, recv.at[R_RGRAD, t], previous)
+        post(rgrad.at[t, other_two], rgrad_in.at[t, two], S_RGRAD, recv.at[R_RGRAD, t], following)
 
     def compute(t):
         @pl.when(t + 1 < STEPS)
@@ -232,9 +239,9 @@
         for kv, (low, other, factor) in enumerate(sides):
             rgrad[t, kv] = (dot(low[768:, :LEAF], other[:LEAF], (1, 0)) * factor).astype(BF16)
             rgrad[t, 2 + kv] = (dot(low[768:, LEAF:], other[LEAF:], (1, 0)) * factor).astype(BF16)
-        two, other_two = pl.ds(0, 2), pl.ds(2, 2)
-        post(rgrad.at[t, two], rgrad_in.at[t, other_two], S_RGRAD, recv.at[R_RGRAD, t], previous)
-        post(rgrad.at[t, other_two], rgrad_in.at[t, two], S_RGRAD, recv.at[R_RGRAD, t], following)
+        @pl.when(t < HOLD)
+        def _():
+            send_rims(t)
 
         for kv, (low, other, factor) in enumerate(sides):
             coarse = dot(low[256:512], other, (1, 0)) * factor
@@ -254,9 +261,16 @@
         )
         return (total + at_rim).T
 
+    def put(t, refs, value):
+        each = STEPS // len(refs)
+        for i, ref in enumerate(refs):
+            @pl.when(lax.div(t, each) == i)
+            def _(ref=ref):
+                ref[:, columns(lax.rem(t, each))] = value
+
     def gather(t):
-        att[:, columns(t)] = gathered(t, 1, v, probs_kept[t]).astype(BF16)
-        gq[:, columns(t)] = gathered(t, 0, k, dscores_kept[t]) * SCALE
+        put(t, (att0, att1), gathered(t, 1, v, probs_kept[t]).astype(BF16))
+        put(t, (gq0, gq1, gq2, gq3), gathered(t, 0, k, dscores_kept[t]) * SCALE)
 
     def halves(t):
         arrived(pgrad_in.at[t], recv.at[R_PGRAD, t])
@@ -280,13 +294,12 @@
         arrived(rgrad_in.at[t], recv.at[R_RGRAD, t])
         arrived(qgrad_in.at[t], recv.at[R_QGRAD, t])
         cols = columns(t)
-        sides = ((dscores_kept, q, gk, gk_out, SCALE), (probs_kept, cot, gv, gv_out, 1.0))
-        for kv, (low, other, out, out_hbm, factor) in enumerate(sides):
+        sides = ((dscores_kept, q, (gk0, gk1, gk2, gk3), SCALE), (probs_kept, cot, (gv0, gv1, gv2, gv3), 1.0))
+        for kv, (low, other, out, factor) in enumerate(sides):
             own = dot(low[t, 0:256, :], other[:, cols], (1, 0)) * factor
             ends = jnp.concatenate([rgrad_in[t, kv], rgrad_in[t, 2 + kv]], axis=0).astype(F32)
             coarse = dot(double, pgrad_in[t, kv, 0:128, :], (1, 0)) + dot(double_twice, qgrad_in[t, kv], (1, 0))
-            out[:, cols] = own + ends + coarse
-            pltpu.make_async_copy(out.at[:, cols], out_hbm.at[:, cols], store.at[kv]).start()
+            put(t, out, own + ends + coarse)
 
     def step(t, carry):
         compute(t)
@@ -318,20 +331,14 @@
     for there, device in plane:
         post(back.at[there], back_in.at[member], S_BACK, plane_recv.at[1], device)
     back_in[member] = back[member]
+    lax.fori_loop(HOLD, STEPS, repeat(send_rims), 0)
 
     lax.fori_loop(0, STEPS, repeat(gather), 0)
-    stores = [
-        pltpu.make_async_copy(src, dst, store.at[2 + i])
-        for i, (src, dst) in enumerate(((att, att_out), (gq, gq_out), (sg, sg_out)))
-    ]
-    stores[0].start()
-    stores[1].start()
     lax.fori_loop(0, STEPS, repeat(join), 0)
     arrived(back_in.at[pl.ds(0, PLANE - 1)], plane_recv.at[1])
     total = jnp.sum(back_in[...].astype(F32), axis=0)
     for c in range(2 * HEADS):
         sg[:, c * HEAD:(c + 1) * HEAD] = total[c:c + 1]
-    stores[2].start()
 
     arrived(tiles_in.at[pl.ds(0, PLANE - 1)], send.at[S_TILE])
     arrived(rim, send.at[S_RIM])
@@ -344,25 +351,21 @@
     arrived(qgrad, send.at[S_QGRAD])
     arrived(sgrad.at[:, pl.ds(0, GROUP - 1)], send.at[S_SGRAD])
     arrived(back.at[pl.ds(0, PLANE - 1)], send.at[S_BACK])
-    arrived(gk, store.at[0])
-    arrived(gv, store.at[1])
-    for copy in stores:
-        copy.wait()
-
-
-def finish(att, gq, gk, gv, sg, att_out, gq_out, gk_out, gv_out, sg_out, kept, low, row, load, store):
-    through = ((sg, row, sg_out), (gk, kept.at[0], gk_out), (gv, kept.at[1], gv_out), (gq, kept.at[2], gq_out), (att, low, att_out))
-    loads = [pltpu.make_async_copy(src, via, load.at[i]) for i, (src, via, _) in enumerate(through)]
-    stores = [pltpu.make_async_copy(via, dst, store.at[i]) for i, (_, via, dst) in enumerate(through)]
-    for copy in loads:
-        copy.start()
-    width = kept.shape[2]
-    for i in range(5):
-        loads[i].wait()
-        if i in (1, 2):
-            kept[i - 1] = kept[i - 1] + row[:, (i - 1) * width:i * width] * (1.0 / 256)
-        stores[i].start()
-    for copy in stores:
+
+
+def finish(*refs):
+    pieces, sg, outs, (kept, sem) = refs[:14], refs[14], refs[15:20], refs[20:]
+    copies = [pltpu.make_async_copy(sg, outs[4], sem.at[14])]
+    copies[0].start()
+    for i, piece in enumerate(pieces):
+        out, at = (outs[0], i) if i < 2 else (outs[1 + (i - 2) // 4], (i - 2) % 4)
+        width = piece.shape[1]
+        if i >= 6:
+            kept[i - 6] = piece[...] + sg[:, (i - 6) * width:(i - 5) * width] * (1.0 / 256)
+            piece = kept.at[i - 6]
+        copies.append(pltpu.make_async_copy(piece, out.at[:, pl.ds(at * width, width)], sem.at[i]))
+        copies[-1].start()
+    for copy in copies:
         copy.wait()
 
 
@@ -377,14 +380,18 @@
         jax.ShapeDtypeStruct((rows, width), F32),
         jax.ShapeDtypeStruct((1, 2 * width), F32),
     )
+    pieces = (
+        [jax.ShapeDtypeStruct((rows, width // 2), BF16)] * 2
+        + [jax.ShapeDtypeStruct((rows, width // 4), F32)] * 12
+        + [jax.ShapeDtypeStruct((1, 2 * width), F32)]
+    )
     block = (STEPS, 4, LEAF, HEAD)
     parts = pl.pallas_call(
         kernel,
-        out_shape=out_shape,
+        out_shape=pieces,
         in_specs=[in_hbm] * 4,
-        out_specs=(in_hbm,) * 5,
-        scratch_shapes=[pltpu.VMEM((rows, width), BF16)] * 5 + [pltpu.VMEM((rows, width), F32)] * 3 + [
-            pltpu.VMEM((1, 2 * width), F32),
+        out_specs=[in_vmem] * 15,
+        scratch_shapes=[pltpu.VMEM((rows, width), BF16)] * 4 + [
             pltpu.VMEM((PLANE, 16, HEAD), BF16),
             pltpu.VMEM((STEPS, GROUP, 64, HEAD), BF16),
             pltpu.VMEM(block, BF16),
@@ -410,26 +417,22 @@
             pltpu.SemaphoreType.DMA((9, STEPS)),
             pltpu.SemaphoreType.DMA((2,)),
             pltpu.SemaphoreType.DMA((4,)),
-            pltpu.SemaphoreType.DMA((5,)),
         ],
         compiler_params=pltpu.CompilerParams(
-            collective_id=0, has_side_effects=True, vmem_limit_bytes=62 * 2**20
+            collective_id=0, has_side_effects=True, vmem_limit_bytes=50 * 2**20
         ),
         name="attend",
     )(queries, keys, values, cotangent)
     return pl.pallas_call(
         finish,
         out_shape=out_shape,
-        in_specs=[in_hbm] * 5,
+        in_specs=[in_vmem] * 15,
         out_specs=(in_hbm,) * 5,
         scratch_shapes=[
-            pltpu.VMEM((3, rows, width), F32),
-            pltpu.VMEM((rows, width), BF16),
-            pltpu.VMEM((1, 2 * width), F32),
-            pltpu.SemaphoreType.DMA((5,)),
-            pltpu.SemaphoreType.DMA((5,)),
+            pltpu.VMEM((8, rows, width // 4), F32),
+            pltpu.SemaphoreType.DMA((15,)),
         ],
-        compiler_params=pltpu.CompilerParams(vmem_limit_bytes=62 * 2**20),
+        compiler_params=pltpu.CompilerParams(vmem_limit_bytes=16 * 2**20),
         name="finish",
     )(*parts)
 

time: 60.6 us -> 59.3 us (0.979)
  Pallas kernels: 59.8 us -> 58.5 us
    pallas_call x2, Pallas kernels: 59.8 us -> 58.5 us  [the longest x1 56.6 us: on_device(): pl.pallas_call(kernel, out_shape=pieces, in_specs=[in_hbm] * 4, out_specs...]
where the time goes in v3:
time: 59.3 us; the launch traced here: 59.2 us
  Pallas kernels  58.5 us (99%)
  between operations  0.64 us (1%)
    pallas_call x1, Pallas kernels, on_device(): pl.pallas_call(kernel, out_shape=pieces, in_specs=[in_hbm] * 4, out_specs...  56.6 us
    pallas_call x1, Pallas kernels, on_device(): pl.pallas_call(finish, out_shape=out_shape, in_specs=[in_vmem] * 15, out_...  1.97 us

profile of v3, /device:TPU:25, one launch (start us, length us, event | category | flops | bytes accessed | tf_op | source)
XLA Modules:
  0.0 59.2 jit_solution(11309260908330395247)
XLA Ops:
  0.6 56.6 %attend.1 = (bf16[256,512]{1,0:T(8,128)(2,1)S(1)}, bf16[256,512]{1,0:T(8,128)(2,1)S(1)}, f32[256,256]{1,0:T(8,128)S(1)}, f32[256,256]{1,0:T(8,128)S(1)}, f32[256...) custom-call(bf16[256,1024]{1,0:T(8,128)(2,1)} %q_in.1, ...), custom_call_target="tpu_custom_call" | custom-call | tf_op jit(solution)/shard_map/attend/pallas_call | solution.py:389
  57.2 2.0 %finish.1 = (bf16[256,1024]{1,0:T(8,128)(2,1)}, f32[256,1024]{1,0:T(8,128)}, f32[256,1024]{1,0:T(8,128)}, f32[256,1024]{1,0:T(8,128)}, f32[1,2048]{1,0:T(1,128)}) custom-call(bf16[256,512]{1,0:T(8,128)(2,1)S(1)} %get-tuple-element.20.refs_0_, bf16[256,512]{1,0:T(8,128)(2,1)S(1)} %get-tuple-element.21.refs_1_, f32[256,256]{1,0:T(8,128)S(1)} %get-tuple-element.22.refs_2_, ...), custom_call_target="tpu_custom_call" | custom-call | tf_op jit(solution)/shard_map/finish/pallas_call | solution.py:426

commit v4 on v3

--- a/solution.py
+++ b/solution.py
@@ -15,7 +15,8 @@
 PLANE = 32
 ZS, YS, XS = 8, 4, 4
 GROUP = 2 * XS
-HOLD = 3
+WINDOW = 3
+HOLD = 4
 HALF_LAG = 2
 POST_LAG = 5
 SCALE = HEAD**-0.5
@@ -25,9 +26,10 @@
 F32 = jnp.float32
 
 (
-    S_TILE, S_RIM, S_PAIR, S_QUAD, S_QFWD, S_SUM, S_RGRAD, S_PGRAD, S_QGRAD, S_SGRAD, S_BACK,
-) = range(11)
-R_RIM, R_PAIR, R_QUAD, R_QFWD, R_SUM, R_RGRAD, R_PGRAD, R_QGRAD, R_SGRAD = range(9)
+    S_TILE, S_RIM, S_PAIR, S_QUAD, S_QFWD, S_SUM, S_SFWD,
+    S_RGRAD, S_PGRAD, S_QGRAD, S_HALF, S_XGRAD, S_BACK,
+) = range(13)
+R_RIM, R_PAIR, R_QUAD, R_QFWD, R_SUM, R_SFWD, R_RGRAD, R_PGRAD, R_QGRAD, R_HALF, R_XGRAD = range(11)
 
 
 def dot(a, b, contract):
@@ -40,7 +42,7 @@
     q, k, v, cot,
     tiles_in, sums, rim, pairs, pairs_in, quads, quads_in,
     rgrad, rgrad_in, pgrad, pgrad_in, qkeep, qgrad, qgrad_in,
-    sgrad, sgrad_in, probs_kept, dscores_kept, stage, back, back_in,
+    sgrad, half_in, xgrad, xgrad_in, probs_kept, dscores_kept, stage, back, back_in,
     send, recv, plane_recv, load,
 ):
     seq, outer = lax.axis_index("seq"), lax.axis_index("outer")
@@ -67,10 +69,9 @@
         if dz or dy
     ]
     group = core * XS + x
-    mates = []
-    for dx, dcore in ((2, 0), (2, 1), (1, 0), (3, 0), (1, 1), (3, 1), (0, 1)):
-        mx, mcore = lax.rem(x + dx, XS), lax.rem(core + dcore, 2)
-        mates.append((mcore * XS + mx, ((mx * 2 + ylo) * 8 + z, yhi * 2 + mcore)))
+    mates = [
+        (there, ((there * 2 + ylo) * 8 + z, outer)) for there in (lax.rem(x + d, XS) for d in (2, 1, 3))
+    ]
 
     loads = [
         pltpu.make_async_copy(src, dst, load.at[i])
@@ -94,6 +95,7 @@
 
     for _, device in plane + mates:
         greet(device)
+    greet(partner)
     greet(following)
     greet(previous)
 
@@ -124,7 +126,7 @@
             quads[t, kv] = quad_rows[:, t * HEAD:(t + 1) * HEAD]
     tiles_in[member] = jnp.concatenate(chunks, axis=0).astype(BF16)
 
-    pl.semaphore_wait(barrier, len(plane) + len(mates) + 2)
+    pl.semaphore_wait(barrier, len(plane) + len(mates) + 3)
 
     for _, device in plane:
         post(tiles_in.at[member], tiles_in.at[member], S_TILE, plane_recv.at[0], device)
@@ -153,11 +155,14 @@
             post(sums.at[t, group], sums.at[t, group], S_SUM, recv.at[R_SUM, t], device)
         return carry
 
-    lax.fori_loop(0, STEPS, send_sums, 0)
+    lax.fori_loop(0, WINDOW, send_sums, 0)
 
     def forward(t):
         arrived(quads_in.at[t, 0], recv.at[R_QUAD, t])
         post(quads_in.at[t, 0], quads_in.at[t, 1], S_QFWD, recv.at[R_QFWD, t], partner)
+        arrived(sums.at[t, pl.ds(0, XS - 1)], recv.at[R_SUM, t])
+        four = sums.at[t, pl.ds(core * XS, XS)]
+        post(four, four, S_SFWD, recv.at[R_SFWD, t], partner)
 
     forward(0)
     loads[2].wait()
@@ -189,6 +194,10 @@
         post(rgrad.at[t, other_two], rgrad_in.at[t, two], S_RGRAD, recv.at[R_RGRAD, t], following)
 
     def compute(t):
+        @pl.when(t + WINDOW < STEPS)
+        def _():
+            send_sums(t + WINDOW, 0)
+
         @pl.when(t + 1 < STEPS)
         def _():
             forward(t + 1)
@@ -196,7 +205,7 @@
         arrived(rim.at[t], recv.at[R_RIM, t])
         arrived(pairs_in.at[t], recv.at[R_PAIR, t])
         arrived(quads_in.at[t, 1], recv.at[R_QFWD, t])
-        arrived(sums.at[t, pl.ds(0, GROUP - 1)], recv.at[R_SUM, t])
+        arrived(sums.at[t, pl.ds(0, XS)], recv.at[R_SFWD, t])
         cols = columns(t)
         qh, ch = q[:, cols], cot[:, cols]
 
@@ -232,9 +241,7 @@
         for kv, (low, other, factor) in enumerate(sides):
             far = (dot(low[512:768], other, (1, 0)) * factor).astype(BF16)
             sgrad[t, :, kv * 32:(kv + 1) * 32, :] = far.reshape(GROUP, 32, HEAD)
-        for there, device in mates:
-            post(sgrad.at[t, there], sgrad_in.at[t, group], S_SGRAD, recv.at[R_SGRAD, t], device)
-        sgrad_in[t, group] = sgrad[t, group]
+        post(sgrad.at[t, pl.ds((1 - core) * XS, XS)], half_in.at[t], S_HALF, recv.at[R_HALF, t], partner)
 
         for kv, (low, other, factor) in enumerate(sides):
             rgrad[t, kv] = (dot(low[768:, :LEAF], other[:LEAF], (1, 0)) * factor).astype(BF16)
@@ -273,13 +280,19 @@
         put(t, (gq0, gq1, gq2, gq3), gathered(t, 0, k, dscores_kept[t]) * SCALE)
 
     def halves(t):
+        arrived(half_in.at[t], recv.at[R_HALF, t])
+        own = sgrad[t, pl.ds(core * XS, XS)].astype(F32)
+        xgrad[t] = (own + half_in[t].astype(F32)).astype(BF16)
+        for there, device in mates:
+            post(xgrad.at[t, there], xgrad_in.at[t, x], S_XGRAD, recv.at[R_XGRAD, t], device)
+        xgrad_in[t, x] = xgrad[t, x]
         arrived(pgrad_in.at[t], recv.at[R_PGRAD, t])
         qgrad[t] = (qkeep[t] + pgrad_in[t, :, 128:192, :].astype(F32)).astype(BF16)
         post(qgrad.at[t], qgrad_in.at[t], S_QGRAD, recv.at[R_QGRAD, t], sibling)
 
     def reduce(t):
-        arrived(sgrad_in.at[t, pl.ds(0, GROUP - 1)], recv.at[R_SGRAD, t])
-        total = jnp.sum(sgrad_in[t].astype(F32), axis=0).astype(BF16)
+        arrived(xgrad_in.at[t, pl.ds(0, XS - 1)], recv.at[R_XGRAD, t])
+        total = jnp.sum(xgrad_in[t].astype(F32), axis=0).astype(BF16)
         for kv in range(2):
             for part in range(2):
                 first = kv * 32 + part * 16
@@ -345,11 +358,13 @@
     arrived(pairs, send.at[S_PAIR])
     arrived(quads, send.at[S_QUAD])
     arrived(quads, send.at[S_QFWD])
-    arrived(sums.at[:, pl.ds(0, GROUP - 1)], send.at[S_SUM])
+    arrived(sums.at[:, pl.ds(0, XS - 1)], send.at[S_SUM])
+    arrived(sums.at[:, pl.ds(0, XS)], send.at[S_SFWD])
     arrived(rgrad, send.at[S_RGRAD])
     arrived(pgrad, send.at[S_PGRAD])
     arrived(qgrad, send.at[S_QGRAD])
-    arrived(sgrad.at[:, pl.ds(0, GROUP - 1)], send.at[S_SGRAD])
+    arrived(half_in, send.at[S_HALF])
+    arrived(xgrad.at[:, pl.ds(0, XS - 1)], send.at[S_XGRAD])
     arrived(back.at[pl.ds(0, PLANE - 1)], send.at[S_BACK])
 
 
@@ -407,14 +422,16 @@
             pltpu.VMEM((STEPS, 2, 64, HEAD), BF16),
             pltpu.VMEM((STEPS, 2, 64, HEAD), BF16),
             pltpu.VMEM((STEPS, GROUP, 64, HEAD), BF16),
-            pltpu.VMEM((STEPS, GROUP, 64, HEAD), BF16),
+            pltpu.VMEM((STEPS, XS, 64, HEAD), BF16),
+            pltpu.VMEM((STEPS, XS, 64, HEAD), BF16),
+            pltpu.VMEM((STEPS, XS, 64, HEAD), BF16),
             pltpu.VMEM((STEPS, 896, 256), BF16),
             pltpu.VMEM((STEPS, 896, 256), BF16),
             pltpu.VMEM((2, 16, 16, HEAD), BF16),
             pltpu.VMEM((PLANE, 16, HEAD), BF16),
             pltpu.VMEM((PLANE, 16, HEAD), BF16),
-            pltpu.SemaphoreType.DMA((11,)),
-            pltpu.SemaphoreType.DMA((9, STEPS)),
+            pltpu.SemaphoreType.DMA((13,)),
+            pltpu.SemaphoreType.DMA((11, STEPS)),
             pltpu.SemaphoreType.DMA((2,)),
             pltpu.SemaphoreType.DMA((4,)),
         ],

time: 59.3 us -> 56.7 us (0.956)
  the two profiles are of different devices: /device:TPU:25 before, /device:TPU:1 now
where the time goes in v4:
time: 56.7 us; the launch traced here: 56.6 us
  Pallas kernels  56 us (99%)
  between operations  0.64 us (1%)
    pallas_call x1, Pallas kernels, on_device(): pl.pallas_call(kernel, out_shape=pieces, in_specs=[in_hbm] * 4, out_specs...  54 us
    pallas_call x1, Pallas kernels, on_device(): pl.pallas_call(finish, out_shape=out_shape, in_specs=[in_vmem] * 15, out_...  1.97 us

profile of v4, /device:TPU:1, one launch (start us, length us, event | category | flops | bytes accessed | tf_op | source)
XLA Modules:
  0.0 56.6 jit_solution(3205174886764381404)
XLA Ops:
  0.6 54.0 %attend.1 = (bf16[256,512]{1,0:T(8,128)(2,1)S(1)}, bf16[256,512]{1,0:T(8,128)(2,1)S(1)}, f32[256,256]{1,0:T(8,128)S(1)}, f32[256,256]{1,0:T(8,128)S(1)}, f32[256...) custom-call(bf16[256,1024]{1,0:T(8,128)(2,1)} %q_in.1, ...), custom_call_target="tpu_custom_call" | custom-call | tf_op jit(solution)/shard_map/attend/pallas_call | solution.py:404
  54.6 2.0 %finish.1 = (bf16[256,1024]{1,0:T(8,128)(2,1)}, f32[256,1024]{1,0:T(8,128)}, f32[256,1024]{1,0:T(8,128)}, f32[256,1024]{1,0:T(8,128)}, f32[1,2048]{1,0:T(1,128)}) custom-call(bf16[256,512]{1,0:T(8,128)(2,1)S(1)} %get-tuple-element.20.refs_0_, bf16[256,512]{1,0:T(8,128)(2,1)S(1)} %get-tuple-element.21.refs_1_, f32[256,256]{1,0:T(8,128)S(1)} %get-tuple-element.22.refs_2_, ...), custom_call_target="tpu_custom_call" | custom-call | tf_op jit(solution)/shard_map/finish/pallas_call | solution.py:443

commit v5 on v4

--- a/solution.py
+++ b/solution.py
@@ -15,7 +15,8 @@
 PLANE = 32
 ZS, YS, XS = 8, 4, 4
 GROUP = 2 * XS
-WINDOW = 3
+AHEAD = 2
+WINDOW = 5
 HOLD = 4
 HALF_LAG = 2
 POST_LAG = 5
@@ -164,7 +165,8 @@
         four = sums.at[t, pl.ds(core * XS, XS)]
         post(four, four, S_SFWD, recv.at[R_SFWD, t], partner)
 
-    forward(0)
+    for t in range(AHEAD):
+        forward(t)
     loads[2].wait()
     loads[3].wait()
 
@@ -198,9 +200,9 @@
         def _():
             send_sums(t + WINDOW, 0)
 
-        @pl.when(t + 1 < STEPS)
+        @pl.when(t + AHEAD < STEPS)
         def _():
-            forward(t + 1)
+            forward(t + AHEAD)
 
         arrived(rim.at[t], recv.at[R_RIM, t])
         arrived(pairs_in.at[t], recv.at[R_PAIR, t])

time: 56.7 us -> 56.1 us (0.989)
  Pallas kernels: 56 us -> 55.4 us
    pallas_call x1, Pallas kernels: 54 us -> 53.4 us  [on_device(): pl.pallas_call(kernel, out_shape=pieces, in_specs=[in_hbm] * 4, out_specs...]
where the time goes in v5:
time: 56.1 us; the launch traced here: 56 us
  Pallas kernels  55.4 us (99%)
  between operations  0.64 us (1%)
    pallas_call x1, Pallas kernels, on_device(): pl.pallas_call(kernel, out_shape=pieces, in_specs=[in_hbm] * 4, out_specs...  53.4 us
    pallas_call x1, Pallas kernels, on_device(): pl.pallas_call(finish, out_shape=out_shape, in_specs=[in_vmem] * 15, out_...  1.97 us

profile of v5, /device:TPU:1, one launch (start us, length us, event | category | flops | bytes accessed | tf_op | source)
XLA Modules:
  0.0 56.0 jit_solution(18229564451198167413)
XLA Ops:
  0.6 53.4 %attend.1 = (bf16[256,512]{1,0:T(8,128)(2,1)S(1)}, bf16[256,512]{1,0:T(8,128)(2,1)S(1)}, f32[256,256]{1,0:T(8,128)S(1)}, f32[256,256]{1,0:T(8,128)S(1)}, f32[256...) custom-call(bf16[256,1024]{1,0:T(8,128)(2,1)} %q_in.1, ...), custom_call_target="tpu_custom_call" | custom-call | tf_op jit(solution)/shard_map/attend/pallas_call | solution.py:406
  54.0 2.0 %finish.1 = (bf16[256,1024]{1,0:T(8,128)(2,1)}, f32[256,1024]{1,0:T(8,128)}, f32[256,1024]{1,0:T(8,128)}, f32[256,1024]{1,0:T(8,128)}, f32[1,2048]{1,0:T(1,128)}) custom-call(bf16[256,512]{1,0:T(8,128)(2,1)S(1)} %get-tuple-element.20.refs_0_, bf16[256,512]{1,0:T(8,128)(2,1)S(1)} %get-tuple-element.21.refs_1_, f32[256,256]{1,0:T(8,128)S(1)} %get-tuple-element.22.refs_2_, ...), custom_call_target="tpu_custom_call" | custom-call | tf_op jit(solution)/shard_map/finish/pallas_call | solution.py:445

commit v6 on v5

--- a/solution.py
+++ b/solution.py
@@ -207,32 +207,32 @@
         arrived(rim.at[t], recv.at[R_RIM, t])
         arrived(pairs_in.at[t], recv.at[R_PAIR, t])
         arrived(quads_in.at[t, 1], recv.at[R_QFWD, t])
-        arrived(sums.at[t, pl.ds(0, XS)], recv.at[R_SFWD, t])
         cols = columns(t)
         qh, ch = q[:, cols], cot[:, cols]
 
-        def against(main, left, right, other):
+        def near(kv, ref, other):
+            main = jnp.concatenate(
+                [ref[:, cols], pairs_in[t, kv], quads_in[t, 0, kv], quads_in[t, 1, kv]], axis=0
+            )
             at_rim = jnp.concatenate(
-                [dot(left, other[:LEAF], (1, 1)), dot(right, other[LEAF:], (1, 1))], axis=1
+                [dot(rim[t, kv], other[:LEAF], (1, 1)), dot(rim[t, 2 + kv], other[LEAF:], (1, 1))], axis=1
             )
-            return jnp.concatenate([dot(main, other, (1, 1)), at_rim], axis=0)
-
-        keys, values = rows_of(t, 0, k), rows_of(t, 1, v)
-        key_l, value_l, key_r, value_r = rim[t, 0], rim[t, 1], rim[t, 2], rim[t, 3]
-        scores = against(keys, key_l, key_r, qh)
+            return dot(main, other, (1, 1)), at_rim
+
+        def far(kv, other):
+            return dot(sums[t, :, kv * 32:(kv + 1) * 32, :].reshape(SPANS, HEAD), other, (1, 1))
+
+        near_scores, rim_scores = near(0, k, qh)
+        near_dprobs, rim_dprobs = near(1, v, ch)
+        arrived(sums.at[t, pl.ds(0, XS)], recv.at[R_SFWD, t])
         scores = jnp.concatenate(
-            [
-                scores[:512],
-                jnp.where(covered, -1e30, scores[512:768]),
-                jnp.where(absent, -1e30, scores[768:]),
-            ],
-            axis=0,
+            [near_scores, jnp.where(covered, -1e30, far(0, qh)), jnp.where(absent, -1e30, rim_scores)], axis=0
         )
         highest = jnp.max(scores, axis=0, keepdims=True)
         weights = jnp.exp2((scores - highest) * (SCALE * LOG2E))
         probs = weights * (1.0 / jnp.sum(weights, axis=0, keepdims=True))
         probs_low = probs.astype(BF16)
-        dprobs = against(values, value_l, value_r, ch)
+        dprobs = jnp.concatenate([near_dprobs, far(1, ch), rim_dprobs], axis=0)
         centre = jnp.sum(probs * dprobs, axis=0, keepdims=True)
         dscores = (probs * (dprobs - centre)).astype(BF16)
 

time: 56.1 us -> 57 us (1.016)
  Pallas kernels: 55.4 us -> 56.3 us
    pallas_call x1, Pallas kernels: 53.4 us -> 54.3 us  [on_device(): pl.pallas_call(kernel, out_shape=pieces, in_specs=[in_hbm] * 4, out_specs...]
where the time goes in v6:
time: 57 us; the launch traced here: 56.9 us
  Pallas kernels  56.3 us (99%)
  between operations  0.64 us (1%)
    pallas_call x1, Pallas kernels, on_device(): pl.pallas_call(kernel, out_shape=pieces, in_specs=[in_hbm] * 4, out_specs...  54.3 us
    pallas_call x1, Pallas kernels, on_device(): pl.pallas_call(finish, out_shape=out_shape, in_specs=[in_vmem] * 15, out_...  1.97 us

profile of v6, /device:TPU:1, one launch (start us, length us, event | category | flops | bytes accessed | tf_op | source)
XLA Modules:
  0.0 56.9 jit_solution(13009872054119599437)
XLA Ops:
  0.6 54.3 %attend.1 = (bf16[256,512]{1,0:T(8,128)(2,1)S(1)}, bf16[256,512]{1,0:T(8,128)(2,1)S(1)}, f32[256,256]{1,0:T(8,128)S(1)}, f32[256,256]{1,0:T(8,128)S(1)}, f32[256...) custom-call(bf16[256,1024]{1,0:T(8,128)(2,1)} %q_in.1, ...), custom_call_target="tpu_custom_call" | custom-call | tf_op jit(solution)/shard_map/attend/pallas_call | solution.py:406
  55.0 2.0 %finish.1 = (bf16[256,1024]{1,0:T(8,128)(2,1)}, f32[256,1024]{1,0:T(8,128)}, f32[256,1024]{1,0:T(8,128)}, f32[256,1024]{1,0:T(8,128)}, f32[1,2048]{1,0:T(1,128)}) custom-call(bf16[256,512]{1,0:T(8,128)(2,1)S(1)} %get-tuple-element.20.refs_0_, bf16[256,512]{1,0:T(8,128)(2,1)S(1)} %get-tuple-element.21.refs_1_, f32[256,256]{1,0:T(8,128)S(1)} %get-tuple-element.22.refs_2_, ...), custom_call_target="tpu_custom_call" | custom-call | tf_op jit(solution)/shard_map/finish/pallas_call | solution.py:445
